TPU v7x, 256 devices: a whole 4x4x8 slice. The times are simulated.
256 devices in a mesh: ctx: 64 (over y, z_lo, x), enc: 4 (over z_hi, core).
Axes of the slice: x: 4, y: 4, z: 8 (z_hi: 2, z_lo: 4; z = z_hi * 4 + z_lo), core: 2. Of those that a mesh axis runs over, the one named last changes fastest.
Arguments:
- qkv: bfloat16 [3, 32768, 4096], P(None, ('ctx', 'enc')), may hold values from -12 to 12
- grad_out: bfloat16 [32768, 4096], P(('ctx', 'enc')), may hold values from -6 to 6
- text_kv: bfloat16 [2, 256, 4096], P(None, 'ctx', 'enc'), may hold values from -12 to 12
- text_len: int32 [1], replicated, may hold values from 128 to 256
- key_tiles: int32 [64, 3], replicated, may hold values from 0 to 63, as said below
- key_count: int32 [64], replicated, may hold values from 2 to 3, as said below
Outputs:
- attn_out: bfloat16 [32768, 4096], P(('ctx', 'enc'))
- grad_q: float32 [32768, 4096], P(('ctx', 'enc'))
- grad_k: float32 [32768, 4096], P(('ctx', 'enc'))
- grad_v: float32 [32768, 4096], P(('ctx', 'enc'))
- grad_text: float32 [2, 256, 4096], P(None, 'ctx', 'enc')
Inputs may be any that keep to these rules, and one draw needn't show every extreme that they name: `key_tiles`: row i lists key tiles of query tile i: its first entry is i, its entries are distinct and within 2 tiles of i. Only the first key_count[i] entries are used; the others are further such tiles. `key_count`: some query tile uses all 3 entries in every draw.
All inputs are finite; a program needn't handle non-finite values.
Results may differ from a plain program's by a relative error of at most 0.012.
Values may be sent and summed in bfloat16 or wider, within the bound.
No kernel may reach another device: no remote copies, remote signals or barrier semaphores. Data moves between devices by JAX's collectives and lax.ppermute only.
A program may use at most 192 MiB of HBM per device.

v0:
```python
import jax
import jax.numpy as jnp
from jax import lax
from jax.sharding import PartitionSpec as P

HD = 128
REACH = 2


MASKED_SCORE = -1e30


def from_behind(block, axis, distance):
    devices = range(lax.axis_size(axis))
    route = [(i - distance, i) for i in devices if i - distance in devices]
    return lax.ppermute(block, axis, route)


def log_norm_of(scores):
    row_max = jnp.max(scores, axis=-1, keepdims=True)
    return row_max + jnp.log(jnp.sum(jnp.exp(scores - row_max), axis=-1, keepdims=True))


def grads_of_scores(scores, value_rows, log_norm, out_dot, grad_rows, inv_root):
    attn_probs = jnp.exp(scores - log_norm[..., None]).astype(jnp.bfloat16)
    prob_grads = jnp.einsum(
        "qhd,khd->hqk", grad_rows, value_rows, preferred_element_type=jnp.float32
    )
    score_grads = (
        inv_root * attn_probs.astype(jnp.float32) * (prob_grads - out_dot[..., None])
    ).astype(jnp.bfloat16)
    return (attn_probs, score_grads)


def shards(qkv, grad_out, text_kv, text_len, key_tiles, key_count):
    inv_root = HD ** (-0.5)
    heads_view, grad_view = (
        lax.all_to_all(qkv, "enc", split_axis=2, concat_axis=1, tiled=True),
        lax.all_to_all(grad_out[None], "enc", split_axis=2, concat_axis=1, tiled=True),
    )
    tok_rows = heads_view.shape[1]
    head_width = heads_view.shape[2]
    head_count = head_width // HD
    slot_total = key_tiles.shape[1]
    queries = heads_view[0].reshape(tok_rows, head_count, HD)
    grad_rows = grad_view[0].reshape(tok_rows, head_count, HD)
    kv_local = heads_view[1:3]
    cycle_pos = lax.axis_index("ctx")
    my_tiles = lax.dynamic_index_in_dim(key_tiles, cycle_pos, 0, keepdims=False)
    my_count = lax.dynamic_index_in_dim(key_count, cycle_pos, 0, keepdims=False)
    received = {0: kv_local}
    from_above = kv_local
    from_below = kv_local
    for offset in range(1, REACH + 1):
        from_above = from_behind(from_above, "ctx", -1)
        from_below = from_behind(from_below, "ctx", 1)
        received[offset] = from_above
        received[-offset] = from_below
    near_tiles = jnp.stack([received[offset] for offset in range(-REACH, REACH + 1)])
    slot_index = my_tiles - cycle_pos + REACH
    slot_blocks = [
        lax.dynamic_index_in_dim(near_tiles, slot_index[slot], 0, keepdims=False)
        for slot in range(slot_total)
    ]
    key_rows = jnp.concatenate([block[0] for block in slot_blocks], 0).reshape(
        slot_total * tok_rows, head_count, HD
    )
    value_rows = jnp.concatenate([block[1] for block in slot_blocks], 0).reshape(
        slot_total * tok_rows, head_count, HD
    )
    key_live = jnp.repeat(jnp.arange(slot_total) < my_count, tok_rows)
    scores = (
        jnp.einsum("qhd,khd->hqk", queries, key_rows, preferred_element_type=jnp.float32) * inv_root
    )
    scores = jnp.where(key_live[None, None, :], scores, MASKED_SCORE)
    self_norm = log_norm_of(scores)[..., 0]
    attn_probs = jnp.exp(scores - self_norm[..., None]).astype(jnp.bfloat16)
    self_out = jnp.einsum(
        "hqk,khd->qhd", attn_probs, value_rows, preferred_element_type=jnp.float32
    )
    text_all = lax.all_gather(text_kv, "ctx", axis=1, tiled=True)
    text_keys = text_all[0].reshape(-1, head_count, HD)
    text_values = text_all[1].reshape(-1, head_count, HD)
    text_live = jnp.arange(text_keys.shape[0]) < text_len[0]
    text_scores = (
        jnp.einsum("qhd,khd->hqk", queries, text_keys, preferred_element_type=jnp.float32)
        * inv_root
    )
    text_scores = jnp.where(text_live[None, None, :], text_scores, MASKED_SCORE)
    text_norm = log_norm_of(text_scores)[..., 0]
    text_probs = jnp.exp(text_scores - text_norm[..., None]).astype(jnp.bfloat16)
    text_out = jnp.einsum(
        "hqk,khd->qhd", text_probs, text_values, preferred_element_type=jnp.float32
    )
    attn_rows = (self_out + text_out).astype(jnp.bfloat16).reshape(tok_rows, head_width)
    attn_out = lax.all_to_all(attn_rows[None], "enc", split_axis=1, concat_axis=2, tiled=True)[0]
    grad_wide = grad_rows.astype(jnp.float32)
    self_dot = jnp.sum(grad_wide * self_out, axis=-1).T
    text_dot = jnp.sum(grad_wide * text_out, axis=-1).T
    _, text_sgrads = grads_of_scores(
        text_scores, text_values, text_norm, text_dot, grad_rows, inv_root
    )
    text_query = jnp.einsum(
        "hqk,khd->qhd", text_sgrads, text_keys, preferred_element_type=jnp.float32
    )
    text_dkey = jnp.einsum("hqk,qhd->khd", text_sgrads, queries, preferred_element_type=jnp.float32)
    text_dvalue = jnp.einsum(
        "hqk,qhd->khd", text_probs, grad_rows, preferred_element_type=jnp.float32
    )
    text_terms = jnp.stack([text_dkey, text_dvalue]).reshape(2, -1, head_width)
    grad_text = lax.psum_scatter(text_terms, "ctx", scatter_dimension=1, tiled=True)
    prob_grads = jnp.einsum(
        "qhd,khd->hqk", grad_rows, value_rows, preferred_element_type=jnp.float32
    )
    score_grads = (
        inv_root * attn_probs.astype(jnp.float32) * (prob_grads - self_dot[..., None])
    ).astype(jnp.bfloat16)
    grad_query = jnp.einsum(
        "hqk,khd->qhd", score_grads, key_rows, preferred_element_type=jnp.float32
    )
    grad_key = jnp.einsum("hqk,qhd->khd", score_grads, queries, preferred_element_type=jnp.float32)
    grad_value = jnp.einsum(
        "hqk,qhd->khd", attn_probs, grad_rows, preferred_element_type=jnp.float32
    )
    terms = jnp.stack(
        [
            grad_key.reshape(slot_total, tok_rows, head_count, HD),
            grad_value.reshape(slot_total, tok_rows, head_count, HD),
        ],
        1,
    ).astype(jnp.bfloat16)
    tile_grads = jnp.zeros((2 * REACH + 1, 2, tok_rows, head_count, HD), jnp.bfloat16)
    for slot in range(slot_total):
        tile_grads = lax.dynamic_update_index_in_dim(tile_grads, terms[slot], slot_index[slot], 0)
    key_grads = tile_grads[REACH].astype(jnp.float32)
    for offset in [step for step in range(-REACH, REACH + 1) if step != 0]:
        key_grads = key_grads + from_behind(tile_grads[REACH + offset], "ctx", offset).astype(
            jnp.float32
        )
    grad_query = grad_query + text_query
    all_grads = jnp.stack([grad_query, key_grads[0], key_grads[1]]).reshape(3, tok_rows, head_width)
    token_grads = lax.all_to_all(all_grads, "enc", split_axis=1, concat_axis=2, tiled=True)
    return (attn_out, token_grads[0], token_grads[1], token_grads[2], grad_text)


def solution(mesh):
    in_specs = (
        P(None, ("ctx", "enc"), None),
        P(("ctx", "enc"), None),
        P(None, "ctx", "enc"),
        P(),
        P(),
        P(),
    )
    out_specs = (
        P(("ctx", "enc"), None),
        P(("ctx", "enc"), None),
        P(("ctx", "enc"), None),
        P(("ctx", "enc"), None),
        P(None, "ctx", "enc"),
    )
    return jax.shard_map(shards, mesh=mesh, in_specs=in_specs, out_specs=out_specs, check_vma=False)
```

profile of v0, /device:TPU:2, one launch (start us, length us, event | category | flops | bytes accessed | tf_op | source)
XLA Modules:
  0.0 1665.1 jit_solution(1376685598666678791)
XLA Ops:
  7.2 7.2 copy.195
  14.4 105.1 %all_to_all.60 = bf16[3,128,4096]{1,0,2:T(4,128)(2,1)} all-to-all(bf16[3,128,4096]{1,0,2:T(4,128)(2,1)} %copy.195), channel_id=1, replica_groups=mesh['ctx'=64,'enc'=4] {'enc'}, dimensions={2} | all-to-all | bytes 6291456 | tf_op jit(solution)/shard_map/all_to_all | solution.py:38
  119.5 7.2 copy.196
  139.8 23.4 %reduce = bf16[4096,128]{1,0:T(8,128)(2,1)S(1)} reduce(bf16[4096,1,128]{2,1,0:T(2,128)(2,1)} %bitcast.140, bf16[]{:T(256)} %broadcast.40), dimensions={1}, to_apply=%bitcast.108.reduce_sub_computation | reduce | bytes 2097154
  174.7 7.0 collective-permute-done
  191.8 5.3 all-to-all-done.2
  204.3 286.1 %all-gather.2.cloned.1.call-done = bf16[2,256,1024]{2,0,1:T(2,128)(2,1)} async-done(((bf16[2,4,1024]{2,0,1:T(2,128)(2,1)}), bf16[2,256,1024]{2,0,1:T(2,128)(2,1)}) %all-gather.2.cloned.1.call-update) | async-done | bytes 1048592 | tf_op jit(solution)/shard_map/all_gather | solution.py:81
  490.5 4.4 fusion.25
  523.4 17.7 %collective-permute-done.3 = bf16[2,512,1024]{1,2,0:T(8,128)(2,1)S(1)} collective-permute-done((bf16[2,512,1024]{1,2,0:T(8,128)(2,1)}, bf16[2,512,1024]{1,2,0:T(8,128)(2,1)S(1)}, u32[]{:S(2)}, u32[]{:S(2)}) %collective-permute-start.3) | collective-permute-done | bytes 2097184 | tf_op jit(solution)/shard_map/ppermute | solution.py:16
  549.6 12.6 bitcast_reduce_fusion
  562.3 10.4 fusion.2
  572.6 5.1 copy-done
  577.7 4.0 fusion.4
  581.8 5.5 convolution_convert_fusion
  587.4 5.3 fusion.10
  592.7 11.9 fusion
  604.7 9.6 convolution_convert_fusion.1
  617.5 4.7 copy.225
  622.2 5.2 broadcast_in_dim.53
  632.0 6.1 slice_bitcast_fusion.3
  645.3 9.4 collective-permute-start.7
  658.6 9.2 reduce.1
  671.5 4.7 all-to-all-start.1
  680.0 5.8 bitcast_add_fusion
  685.8 8.1 collective-permute-done.4
  693.9 36.7 %collective-permute-done.5 = bf16[2,512,8,128]{1,3,2,0:T(8,128)(2,1)} collective-permute-done((bf16[2,512,8,128]{1,3,2,0:T(8,128)(2,1)}, bf16[2,512,8,128]{1,3,2,0:T(8,128)(2,1)}, u32[]{:S(2)}, u32[]{:S(2)}) %collective-permute-start.5) | collective-permute-done | bytes 2097184 | tf_op jit(solution)/shard_map/ppermute | solution.py:16
  730.7 6.1 collective-permute-done.7
  736.8 5.8 fusion.7
  746.0 9.7 copy.226
  755.7 5.7 all-to-all-start.3
  775.8 859.7 %all-reduce.3.cloned.1.call-done = f32[2,256,1024]{2,1,0:T(8,128)} async-done(((f32[2,256,1024]{2,1,0:T(8,128)}), f32[2,256,1024]{2,1,0:T(8,128)}) %all-reduce.3.cloned.1.call-update) | async-done | bytes 2097168
  1636.9 7.0 copy.227
  (129 shorter events, 131.2 us)
Async XLA Ops:
  7.2 483.3 %all-gather.2.cloned.1.call-start = ((), (), s32[]{:S(2)}) async-start(), calls=%async_computation.4 | async-start | bytes 1064960 | tf_op jit(solution)/shard_map/all_gather | solution.py:81
  126.7 7.9 copy-start.20
  126.7 8.6 copy-start.14
  131.2 50.5 %collective-permute-start = (bf16[2,512,1024]{1,2,0:T(8,128)(2,1)}, bf16[2,512,1024]{1,2,0:T(8,128)(2,1)}, u32[]{:S(2)}, u32[]{:S(2)}) collective-permute-start(bf16[2,512,1024]{1,2,0:T(8,128)(2,1)} %copy.254), channel_id=1, source_target_pairs={{0,4},{4,8},{8,12},{12,16},{16,20},{20,24},{24,28},{28,32},{32,36}... | collective-permute-start | bytes 6291464 | tf_op jit(solution)/shard_map/ppermute | solution.py:16
  139.2 33.6 %copy-start.22 = (s32[64]{0:T(128)S(1)}, s32[64]{0:T(128)}, u32[]{:S(2)}) copy-start(s32[64]{0:T(128)} %param.11) | copy-start | bytes 772
  139.2 34.9 %copy-start.21 = (s32[64,3]{0,1:T(4,128)S(1)}, s32[64,3]{0,1:T(4,128)}, u32[]{:S(2)}) copy-start(s32[64,3]{0,1:T(4,128)} %param.10) | copy-start | bytes 2308
  164.8 32.2 %all-to-all-start.2 = ((bf16[4,2,65536]{2,1,0:T(2,128)(2,1)}), bf16[4,2,65536]{2,1,0:T(2,128)(2,1)S(1)}, u32[]{:S(2)}, u32[]{:S(2)}) async-start(bf16[4,2,65536]{2,1,0:T(2,128)(2,1)} %reshape.100), calls=%async_computation.2 | async-start | bytes 2097152 | tf_op jit(solution)/shard_map/all_to_all | solution.py:39
  168.4 344.4 %collective-permute-start.2 = (bf16[2,512,1024]{1,2,0:T(8,128)(2,1)}, bf16[2,512,1024]{1,2,0:T(8,128)(2,1)}, u32[]{:S(2)}, u32[]{:S(2)}) collective-permute-start(bf16[2,512,1024]{1,2,0:T(8,128)(2,1)} %copy.254), channel_id=1, source_target_pairs={{4,0},{8,4},{12,8},{16,12},{20,16},{24,20},{28,24},{32,28},{36,32}... | collective-permute-start | bytes 6291464 | tf_op jit(solution)/shard_map/ppermute | solution.py:16
  181.7 336.2 %collective-permute-start.1 = (bf16[2,512,1024]{1,2,0:T(8,128)(2,1)}, bf16[2,512,1024]{1,2,0:T(8,128)(2,1)}, u32[]{:S(2)}, u32[]{:S(2)}) collective-permute-start(bf16[2,512,1024]{1,2,0:T(8,128)(2,1)} %collective-permute-done), channel_id=1, source_target_pairs={{0,4},{4,8},{8,12},{12,16},{16,20},{20,24},{24,28},{28,32},{32,36}... | collective-permute-start | bytes 6291464 | tf_op jit(solution)/shard_map/ppermute | solution.py:16
  204.3 388.4 %copy-start.6 = (bf16[512,8,128]{0,2,1:T(8,128)(2,1)}, bf16[512,8,128]{0,2,1:T(8,128)(2,1)S(1)}, u32[]{:S(2)}) copy-start(bf16[512,8,128]{0,2,1:T(8,128)(2,1)S(1)} %reshape_squeeze.15) | copy-start | bytes 3145732
  506.5 4.2 copy-start.11
  510.7 39.0 %copy-start.8 = (bf16[512,8,128]{0,2,1:T(8,128)(2,1)}, bf16[512,8,128]{0,2,1:T(8,128)(2,1)S(1)}, u32[]{:S(2)}) copy-start(bf16[512,8,128]{0,2,1:T(8,128)(2,1)S(1)} %copy.232) | copy-start | bytes 3145732
  512.8 28.3 %collective-permute-start.3 = (bf16[2,512,1024]{1,2,0:T(8,128)(2,1)}, bf16[2,512,1024]{1,2,0:T(8,128)(2,1)S(1)}, u32[]{:S(2)}, u32[]{:S(2)}) collective-permute-start(bf16[2,512,1024]{1,2,0:T(8,128)(2,1)} %collective-permute-done.2), channel_id=1, source_target_pairs={{4,0},{8,4},{12,8},{16,12},{20,16},{24,20},{28,24},{32,28},{36,32}... | collective-permute-start | bytes 6291464 | tf_op jit(solution)/shard_map/ppermute | solution.py:16
  515.8 3.9 copy-start.2
  562.3 15.5 copy-start
  581.8 5.6 copy-start.5
  581.8 5.6 copy-start.19
  592.7 11.9 copy-start.9
  622.2 5.2 copy-start.1
  632.0 22.8 %copy-start.15 = (bf16[512,8,128]{0,2,1:T(8,128)(2,1)S(1)}, bf16[512,8,128]{0,2,1:T(8,128)(2,1)}, u32[]{:S(2)}) copy-start(bf16[512,8,128]{0,2,1:T(8,128)(2,1)} %get-tuple-element.40) | copy-start | bytes 3145732
  638.0 55.9 %collective-permute-start.4 = (bf16[2,512,8,128]{1,3,2,0:T(8,128)(2,1)}, bf16[2,512,8,128]{1,3,2,0:T(8,128)(2,1)}, u32[]{:S(2)}, u32[]{:S(2)}) collective-permute-start(bf16[2,512,8,128]{1,3,2,0:T(8,128)(2,1)} %get-tuple-element.27), channel_id=1, source_target_pairs={{8,0},{12,4},{16,8},{20,12},{24,16},{28,20},{32,24},{36,28},{40,32... | collective-permute-start | bytes 6291464 | tf_op jit(solution)/shard_map/ppermute | solution.py:16
  639.3 91.4 %collective-permute-start.5 = (bf16[2,512,8,128]{1,3,2,0:T(8,128)(2,1)}, bf16[2,512,8,128]{1,3,2,0:T(8,128)(2,1)}, u32[]{:S(2)}, u32[]{:S(2)}) collective-permute-start(bf16[2,512,8,128]{1,3,2,0:T(8,128)(2,1)} %get-tuple-element.30), channel_id=1, source_target_pairs={{4,0},{8,4},{12,8},{16,12},{20,16},{24,20},{28,24},{32,28},{36,32}... | collective-permute-start | bytes 6291464 | tf_op jit(solution)/shard_map/ppermute | solution.py:16
  641.3 89.4 %collective-permute-start.6 = (bf16[2,512,8,128]{1,3,2,0:T(8,128)(2,1)}, bf16[2,512,8,128]{1,3,2,0:T(8,128)(2,1)}, u32[]{:S(2)}, u32[]{:S(2)}) collective-permute-start(bf16[2,512,8,128]{1,3,2,0:T(8,128)(2,1)} %get-tuple-element.29), channel_id=1, source_target_pairs={{0,4},{4,8},{8,12},{12,16},{16,20},{20,24},{24,28},{28,32},{32,36}... | collective-permute-start | bytes 6291464 | tf_op jit(solution)/shard_map/ppermute | solution.py:16
  645.3 91.5 %collective-permute-start.7 = (bf16[2,512,8,128]{1,3,2,0:T(8,128)(2,1)}, bf16[2,512,8,128]{1,3,2,0:T(8,128)(2,1)}, u32[]{:S(2)}, u32[]{:S(2)}) collective-permute-start(bf16[2,512,8,128]{1,3,2,0:T(8,128)(2,1)} %get-tuple-element.28), channel_id=1, source_target_pairs={{0,8},{4,12},{8,16},{12,20},{16,24},{20,28},{24,32},{28,36},{32,40... | collective-permute-start | bytes 6291464 | tf_op jit(solution)/shard_map/ppermute | solution.py:16
  658.6 17.6 %copy-start.3 = (bf16[8,512,256]{1,2,0:T(8,128)(2,1)S(1)}, bf16[8,512,256]{1,2,0:T(8,128)(2,1)}, u32[]{:S(2)}) copy-start(bf16[8,512,256]{1,2,0:T(8,128)(2,1)} %copy-done.2) | copy-start | bytes 6291460
  658.6 17.6 %copy-start.7 = (bf16[512,8,128]{0,2,1:T(8,128)(2,1)S(1)}, bf16[512,8,128]{0,2,1:T(8,128)(2,1)}, u32[]{:S(2)}) copy-start(bf16[512,8,128]{0,2,1:T(8,128)(2,1)} %copy-done.6) | copy-start | bytes 3145732
  671.5 84.2 %all-to-all-start.1 = ((bf16[4,2,65536]{2,1,0:T(2,128)(2,1)}), bf16[4,2,65536]{2,1,0:T(2,128)(2,1)}, u32[]{:S(2)}, u32[]{:S(2)}) async-start(bf16[4,2,65536]{2,1,0:T(2,128)(2,1)} %reshape.98), calls=%async_computation.1 | async-start | bytes 2097152 | tf_op jit(solution)/shard_map/all_to_all | solution.py:96
  676.2 3.8 copy-start.16
  676.2 3.8 copy-start.17
  676.2 3.8 copy-start.18
  755.7 881.2 %all-to-all-start.3 = ((f32[3,512,1024]{2,0,1:T(4,128)}), f32[3,512,1024]{2,0,1:T(4,128)}, u32[]{:S(2)}, u32[]{:S(2)}) async-start(f32[3,512,1024]{2,0,1:T(4,128)} %copy.226), calls=%async_computation.3 | async-start | bytes 16777216 | tf_op jit(solution)/shard_map/all_to_all | solution.py:142
  761.4 874.1 %all-reduce.3.cloned.1.call-start = ((), (), s32[]{:S(2)}) async-start(), calls=%async_computation.5 | async-start | bytes 4194304
  (5 other events, 13.3 us)
Sparse Core Ops, SparseCore 0:
  135.4 355.0 all-gather.1
  769.4 865.9 all-reduce.2
where the time goes:
time: 1670 us
  waiting for transfers between devices  1230 us (74%)
  local copies, waits for them, and re-layouts  141 us (8%)
  blocking collectives  105 us (6%)
  other arithmetic  64.9 us (4%)
  matrix products  60.9 us (4%)
  starting transfers between devices  43.8 us (3%)
  between operations  22.1 us (1%)
    unnamed x3, waiting for transfers between devices  860 us
    all_gather x1, waiting for transfers between devices, shards(): text_all = lax.all_gather(text_kv, 'ctx', axis=1, tiled=True)  286 us
    all_to_all x1, blocking collectives, shards(): lax.all_to_all(qkv, 'enc', split_axis=2, concat_axis=1, tiled=True)  105 us
    ppermute x8, waiting for transfers between devices, from_behind(): return lax.ppermute(block, axis, route)  75.6 us
    unnamed x69, local copies, waits for them, and re-layouts  47.8 us
  transfers between devices with their start and end apart: 13, of which 8 were waited for; matrix products, arithmetic and copies ran while one was open for 8% of the time, Pallas kernels for 0%

commit v1 on v0

v1 whole, which is shorter than its diff:
```python
import math

import jax
import jax.numpy as jnp
from jax import lax
from jax.experimental import pallas as pl
from jax.experimental.pallas import tpu as pltpu
from jax.sharding import PartitionSpec as P

HD = 128
REACH = 2
OFFSETS = (0, 1, -1, 2, -2)
MASKED_SCORE = -1e30
ROOT = HD ** (-0.5)
LOG2E = math.log2(math.e)
F32 = jnp.float32
BF16 = jnp.bfloat16


def nt(a, b):
    return lax.dot_general(a, b, (((1,), (1,)), ((), ())), preferred_element_type=F32)


def nn(a, b):
    return lax.dot_general(a, b, (((1,), (0,)), ((), ())), preferred_element_type=F32)


def tn(a, b):
    return lax.dot_general(a, b, (((0,), (0,)), ((), ())), preferred_element_type=F32)


def fold8(op, x):
    return op(x.reshape(x.shape[0] // 8, 8, x.shape[1]), axis=0)


def attention_kernel(meta, *refs):
    n = len(OFFSETS)
    qg = refs[0:2]
    kv = [refs[2 + 2 * i : 4 + 2 * i] for i in range(n)]
    text = refs[2 + 2 * n]
    outs = refs[3 + 2 * n :]
    out_q = outs[0:2]
    out_kv = [outs[2 + 2 * i : 4 + 2 * i] for i in range(n)]
    out_text = outs[2 + 2 * n]
    q_s, g_s, gt_s, s_s, p_s, top_s, sum_s, acc_s = outs[3 + 2 * n :]
    half = qg[0].shape[1]
    text_rows = text.shape[1]

    for h in range(2):
        q_s[h * half : (h + 1) * half] = qg[h][0]
        g_s[h * half : (h + 1) * half] = qg[h][1]
    gt_s[...] = g_s[...].astype(F32).T
    scale2 = ROOT * LOG2E

    row = lax.broadcasted_iota(jnp.int32, (text_rows, 1), 0)
    live = (row ^ meta[n + 1]) < meta[n]
    ts = jnp.where(live, nt(text[0], q_s[...]), MASKED_SCORE)
    ttop = jnp.max(ts, axis=0, keepdims=True)
    te = jnp.exp2((ts - ttop) * scale2)
    tp = (te * (1.0 / jnp.sum(te, axis=0, keepdims=True))).astype(BF16)
    tout = tn(text[1], tp)
    tdot = jnp.sum(tout * gt_s[...], axis=0, keepdims=True)
    out_text[1] = nn(tp, g_s[...]).astype(out_text.dtype)
    tds = (tp.astype(F32) * (nt(text[1], g_s[...]) - tdot)).astype(BF16)
    out_text[0] = (nn(tds, q_s[...]) * ROOT).astype(out_text.dtype)
    acc_s[1] = tn(text[0], tds)

    def scores(i):
        for h in range(2):
            s = nt(kv[i][h][0], q_s[...])
            s_s[i, h * half : (h + 1) * half] = s
            top = fold8(jnp.max, s)
            if i == 0 and h == 0:
                top_s[...] = top
            else:
                top_s[...] = jnp.maximum(top_s[...], top)

    def exps(i):
        top = jnp.max(top_s[...], axis=0, keepdims=True)
        for h in range(2):
            e = jnp.exp2((s_s[i, h * half : (h + 1) * half] - top) * scale2)
            s_s[i, h * half : (h + 1) * half] = e
            part = fold8(jnp.sum, e)
            if i == 0 and h == 0:
                sum_s[...] = part
            else:
                sum_s[...] += part

    def values(i):
        inverse = 1.0 / jnp.sum(sum_s[...], axis=0, keepdims=True)
        for h in range(2):
            p = (s_s[i, h * half : (h + 1) * half] * inverse).astype(BF16)
            p_s[i, h * half : (h + 1) * half] = p
            o = tn(kv[i][h][1], p)
            if i == 0 and h == 0:
                acc_s[0] = o
            else:
                acc_s[0] += o
            out_kv[i][h][1] = nn(p, g_s[...]).astype(BF16)

    def grads(i):
        dot = top_s[0:1]
        for h in range(2):
            dp = nt(kv[i][h][1], g_s[...])
            p = p_s[i, h * half : (h + 1) * half].astype(F32)
            ds = (p * (dp - dot)).astype(BF16)
            out_kv[i][h][0] = (nn(ds, q_s[...]) * ROOT).astype(BF16)
            acc_s[1] += tn(kv[i][h][0], ds)

    def each(step):
        step(0)
        for i in range(1, n):
            pl.when(meta[i] > 0)(lambda i=i: step(i))

    each(scores)
    each(exps)
    each(values)
    self_out = acc_s[0]
    top_s[0:1] = jnp.sum(self_out * gt_s[...], axis=0, keepdims=True)
    rows_out = (self_out + tout).T.astype(BF16)
    each(grads)
    for i in range(1, n):

        @pl.when(meta[i] == 0)
        def _():
            for h in range(2):
                out_kv[i][h][...] = jnp.zeros_like(out_kv[i][h])

    rows_dq = (acc_s[1] * ROOT).T.astype(BF16)
    for h in range(2):
        out_q[h][0] = rows_out[h * half : (h + 1) * half]
        out_q[h][1] = rows_dq[h * half : (h + 1) * half]


def attention(meta, qg, kv, text):
    half, width = qg[0].shape[1:]
    heads = width // HD
    rows = 2 * half
    text_rows = text.shape[1]
    n = len(OFFSETS)
    tile = pl.BlockSpec((2, half, HD), lambda h, meta: (0, 0, h))
    text_tile = pl.BlockSpec((2, text_rows, HD), lambda h, meta: (0, 0, h))
    part = jax.ShapeDtypeStruct((2, half, width), BF16)
    keys = 3 * rows + text_rows
    return pl.pallas_call(
        attention_kernel,
        grid_spec=pltpu.PrefetchScalarGridSpec(
            num_scalar_prefetch=1,
            grid=(heads,),
            in_specs=[tile] * (2 + 2 * n) + [text_tile],
            out_specs=[tile] * (2 + 2 * n) + [text_tile],
            scratch_shapes=[
                pltpu.VMEM((rows, HD), BF16),
                pltpu.VMEM((rows, HD), BF16),
                pltpu.VMEM((HD, rows), F32),
                pltpu.VMEM((n, rows, rows), F32),
                pltpu.VMEM((n, rows, rows), BF16),
                pltpu.VMEM((8, rows), F32),
                pltpu.VMEM((8, rows), F32),
                pltpu.VMEM((2, HD, rows), F32),
            ],
        ),
        out_shape=[part] * (2 + 2 * n) + [jax.ShapeDtypeStruct((2, text_rows, width), BF16)],
        compiler_params=pltpu.CompilerParams(vmem_limit_bytes=48 * 2**20),
        cost_estimate=pl.CostEstimate(
            flops=12 * heads * rows * keys * HD,
            bytes_accessed=2 * (4 + 4 * n + 2) * half * width * 2,
            transcendentals=heads * rows * keys,
        ),
        name="attention",
    )(meta, *qg, *[part for pair in kv for part in pair], text)


def place_kernel(meta, *refs):
    pieces = refs[0:4]
    outs = refs[4:]
    width = pieces[0].shape[2]
    for m in range(4):
        start = pl.multiple_of((meta[0] ^ m) * width, width)
        for i, out in enumerate(outs):
            out[:, pl.ds(start, width)] = pieces[m][i].astype(out.dtype)


def place(enc, pieces, dtypes):
    _, rows, width = pieces[0].shape
    return pl.pallas_call(
        place_kernel,
        in_specs=[pl.BlockSpec(memory_space=pltpu.SMEM)] + [pl.BlockSpec(memory_space=pltpu.VMEM)] * 4,
        out_specs=[pl.BlockSpec(memory_space=pltpu.VMEM)] * len(dtypes),
        out_shape=[jax.ShapeDtypeStruct((rows, 4 * width), d) for d in dtypes],
        compiler_params=pltpu.CompilerParams(vmem_limit_bytes=24 * 2**20),
        cost_estimate=pl.CostEstimate(flops=0, bytes_accessed=rows * width * 4 * 12, transcendentals=0),
        name="place",
    )(enc, *pieces)


def shards(qkv, grad_out, text_kv, text_len, key_tiles, key_count):
    ctx_size, enc_size = lax.axis_size("ctx"), lax.axis_size("enc")
    ctx, enc = lax.axis_index("ctx"), lax.axis_index("enc")
    width = qkv.shape[2] // enc_size
    rows = qkv.shape[1]

    def send(block, target):
        route = []
        for c in range(ctx_size):
            for e in range(enc_size):
                to = target(c, e)
                if 0 <= to[0] < ctx_size:
                    route.append((c * enc_size + e, to[0] * enc_size + to[1]))
        return lax.ppermute(block, ("ctx", "enc"), route)

    def swap(block, m):
        return send(block, lambda c, e: (c, e ^ m))

    def shift(block, d):
        return send(block, lambda c, e: (c + d, e))

    def across(block, m):
        return send(block, lambda c, e: (c ^ m, e))

    def columns(block, m):
        return lax.dynamic_slice_in_dim(block, (enc ^ m) * width, width, block.ndim - 1)

    kv_own = qkv[1:3]
    kv_in = [swap(columns(kv_own, m), m) if m else columns(kv_own, m) for m in range(4)]
    kv_halves = [jnp.concatenate(kv_in[0:2], 1), jnp.concatenate(kv_in[2:4], 1)]
    near = {0: kv_halves, 1: [None, None], -1: [None, None], 2: [None, None], -2: [None, None]}
    for h in range(2):
        for sign in (1, -1):
            near[sign][h] = shift(kv_halves[h], -sign)
        for sign in (1, -1):
            near[2 * sign][h] = shift(near[sign][h], -sign)

    def qg_columns(m):
        return jnp.stack([columns(qkv[0], m), columns(grad_out, m)])

    qg_in = [swap(qg_columns(m), m) if m else qg_columns(m) for m in range(4)]
    qg = [jnp.concatenate(qg_in[0:2], 1), jnp.concatenate(qg_in[2:4], 1)]

    text = text_kv
    for step in (1, 4, 16):
        text = jnp.concatenate([text] + [across(text, m * step) for m in (1, 2, 3)], 1)

    my_tiles = lax.dynamic_index_in_dim(key_tiles, ctx, 0, keepdims=False)
    my_count = lax.dynamic_index_in_dim(key_count, ctx, 0, keepdims=False)
    listed = jnp.arange(my_tiles.shape[0]) < my_count
    meta = jnp.stack(
        [jnp.any(listed & (my_tiles - ctx == o)).astype(jnp.int32) for o in OFFSETS]
        + [text_len[0], ctx * text_kv.shape[1]]
    ).astype(jnp.int32)

    outs = attention(meta, qg, [near[o] for o in OFFSETS], text)
    out_q = outs[0:2]
    terms = {o: outs[2 + 2 * i : 4 + 2 * i] for i, o in enumerate(OFFSETS)}
    text_terms = outs[2 + 2 * len(OFFSETS)]

    grad_halves = [None, None]
    for h in (1, 0):
        total = terms[0][h].astype(F32)
        for sign in (1, -1):
            far = shift(terms[2 * sign][h], sign)
            mid = (terms[sign][h].astype(F32) + far.astype(F32)).astype(BF16)
            total = total + shift(mid, sign).astype(F32)
        grad_halves[h] = total.astype(BF16)

    def back(halves):
        pieces = []
        for m in range(4):
            piece = halves[m // 2][:, (m % 2) * rows : (m % 2 + 1) * rows]
            pieces.append(swap(piece, m) if m else piece)
        return pieces

    meta_enc = enc.astype(jnp.int32).reshape(1)
    attn_out, grad_q = place(meta_enc, back(out_q), (BF16, F32))
    grad_k, grad_v = place(meta_enc, back(grad_halves), (F32, F32))

    grad_text = text_terms
    for step in (16, 4, 1):
        size = grad_text.shape[1] // 4
        total = grad_text[:, 0:size].astype(F32)
        for m in (1, 2, 3):
            total = total + across(grad_text[:, m * size : (m + 1) * size], m * step).astype(F32)
        grad_text = total if step == 1 else total.astype(BF16)
    return (attn_out, grad_q, grad_k, grad_v, grad_text)


def solution(mesh):
    in_specs = (
        P(None, ("ctx", "enc"), None),
        P(("ctx", "enc"), None),
        P(None, "ctx", "enc"),
        P(),
        P(),
        P(),
    )
    out_specs = (
        P(("ctx", "enc"), None),
        P(("ctx", "enc"), None),
        P(("ctx", "enc"), None),
        P(("ctx", "enc"), None),
        P(None, "ctx", "enc"),
    )
    return jax.shard_map(shards, mesh=mesh, in_specs=in_specs, out_specs=out_specs, check_vma=False)
```

time: 1670 us -> 587 us (0.35)
  the two profiles are of different devices: /device:TPU:2 before, /device:TPU:42 now
where the time goes in v1:
time: 587 us; the launch traced here: 593 us
  starting transfers between devices  404 us (69%)
  waiting for transfers between devices  116 us (20%)
  Pallas kernels  41.5 us (7%)
  local copies, waits for them, and re-layouts  13.3 us (2%)
  other arithmetic  12.5 us (2%)
    ppermute x46, starting transfers between devices, send(): return lax.ppermute(block, ('ctx', 'enc'), route)  404 us
    ppermute x46, waiting for transfers between devices, send(): return lax.ppermute(block, ('ctx', 'enc'), route)  116 us
    pallas_call x1, Pallas kernels, attention(): pl.pallas_call(attention_kernel, grid_spec=pltpu.PrefetchScalarGridSpec(n...  37.4 us
  transfers between devices with their start and end apart: 46, of which 11 were waited for; matrix products, arithmetic and copies ran while one was open for 4% of the time, Pallas kernels for 0%

profile of v1, /device:TPU:42, one launch (start us, length us, event | category | flops | bytes accessed | tf_op | source)
XLA Modules:
  0.0 593.0 jit_solution(11492435981014441131)
XLA Ops:
  3.4 6.3 %collective-permute-start.4 = (bf16[2,128,1024]{2,1,0:T(8,128)(2,1)}, bf16[2,128,1024]{2,1,0:T(8,128)(2,1)S(1)}, u32[]{:S(2)}, u32[]{:S(2)}) collective-permute-start(bf16[2,128,1024]{2,1,0:T(8,128)(2,1)} %get-tuple-element.45), channel_id=1, source_target_pairs={{0,2},{1,3},{2,0},{3,1},{4,6},{5,7},{6,4},{7,5},{8,10},{9,11},{10,... | collective-permute-start | bytes 1572872 | tf_op jit(solution)/shard_map/ppermute | solution.py:210
  13.8 2.7 collective-permute-done.15
  17.7 2.4 collective-permute-start.18
  20.0 40.5 %collective-permute-done.19 = bf16[2,16,1024]{2,1,0:T(8,128)(2,1)S(1)} collective-permute-done((bf16[2,16,1024]{2,1,0:T(8,128)(2,1)S(1)}, bf16[2,16,1024]{2,1,0:T(8,128)(2,1)S(1)}, u32[]{:S(2)}, u32[]{:S(2)}) %collective-permute-start.19) | collective-permute-done | bytes 65568 | tf_op jit(solution)/shard_map/ppermute | solution.py:210
  60.9 4.0 collective-permute-done.17
  69.6 3.5 collective-permute-start.8
  73.1 2.4 collective-permute-start.6
  75.7 3.4 collective-permute-start.9
  79.1 3.1 collective-permute-start.7
  84.2 4.7 collective-permute-done.20
  89.0 26.3 %collective-permute-done.2 = bf16[2,128,1024]{2,1,0:T(8,128)(2,1)S(1)} collective-permute-done((bf16[2,128,1024]{2,1,0:T(8,128)(2,1)S(1)}, bf16[2,128,1024]{2,1,0:T(8,128)(2,1)S(1)}, u32[]{:S(2)}, u32[]{:S(2)}) %collective-permute-start.2) | collective-permute-done | bytes 524320 | tf_op jit(solution)/shard_map/ppermute | solution.py:210
  115.3 3.7 collective-permute-start.1
  120.9 30.3 %collective-permute-start.10 = (bf16[2,256,1024]{2,1,0:T(8,128)(2,1)}, bf16[2,256,1024]{2,1,0:T(8,128)(2,1)}, u32[]{:S(2)}, u32[]{:S(2)}) collective-permute-start(bf16[2,256,1024]{2,1,0:T(8,128)(2,1)} %collective-permute-done.6.refs_4_), channel_id=1, source_target_pairs={{4,0},{5,1},{6,2},{7,3},{8,4},{9,5},{10,6},{11,7},{12,8},{13,9},{1... | collective-permute-start | bytes 3145736 | tf_op jit(solution)/shard_map/ppermute | solution.py:210
  153.2 6.0 %collective-permute-start.11 = (bf16[2,256,1024]{2,1,0:T(8,128)(2,1)}, bf16[2,256,1024]{2,1,0:T(8,128)(2,1)}, u32[]{:S(2)}, u32[]{:S(2)}) collective-permute-start(bf16[2,256,1024]{2,1,0:T(8,128)(2,1)} %collective-permute-done.7.refs_5_), channel_id=1, source_target_pairs={{4,0},{5,1},{6,2},{7,3},{8,4},{9,5},{10,6},{11,7},{12,8},{13,9},{1... | collective-permute-start | bytes 3145736 | tf_op jit(solution)/shard_map/ppermute | solution.py:210
  170.1 7.2 %concatenate.29.refs_12_ = bf16[2,256,1024]{2,1,0:T(8,128)(2,1)} concatenate(bf16[2,4,1024]{2,1,0:T(4,128)(2,1)S(1)} %copy-done.10, bf16[2,4,1024]{2,1,0:T(4,128)(2,1)S(1)} %collective-permute-done.14, bf16[2,4,1024]{2,1,0:T(4,128)(2,1)S(1)} %collective-permute-done.15, bf16[2,4,1024]{2,1,0:T(4,128)(2,1)S(1)} %collective-permute-done.16, ...), dimensions={1} | concatenate | bytes 2097152 | tf_op jit(solution)/shard_map/concatenate | solution.py:242
  179.4 14.8 %collective-permute-done.13.refs_11_ = bf16[2,256,1024]{2,1,0:T(8,128)(2,1)} collective-permute-done((bf16[2,256,1024]{2,1,0:T(8,128)(2,1)}, bf16[2,256,1024]{2,1,0:T(8,128)(2,1)}, u32[]{:S(2)}, u32[]{:S(2)}) %collective-permute-start.13) | collective-permute-done | bytes 1048608 | tf_op jit(solution)/shard_map/ppermute | solution.py:210
  196.0 37.4 %attention.1 = (bf16[2,256,1024]{2,1,0:T(8,128)(2,1)S(1)}, bf16[2,256,1024]{2,1,0:T(8,128)(2,1)S(1)}, bf16[2,256,1024]{2,1,0:T(8,128)(2,1)S(1)}, bf16[2,256,1024...) custom-call(s32[7]{0:T(128)S(1)} %stack.75.meta, ...), custom_call_target="tpu_custom_call" | custom-call | flops 11274289152 | bytes 27262976 | tf_op jit(solution)/shard_map/attention/pallas_call | solution.py:145
  240.8 30.1 %collective-permute-start.28 = (bf16[2,256,1024]{2,1,0:T(8,128)(2,1)}, bf16[2,256,1024]{2,1,0:T(8,128)(2,1)S(1)}, u32[]{:S(2)}, u32[]{:S(2)}) collective-permute-start(bf16[2,256,1024]{2,1,0:T(8,128)(2,1)} %get-tuple-element.30), channel_id=1, source_target_pairs={{4,0},{5,1},{6,2},{7,3},{8,4},{9,5},{10,6},{11,7},{12,8},{13,9},{1... | collective-permute-start | bytes 3145736 | tf_op jit(solution)/shard_map/ppermute | solution.py:210
  273.0 9.6 %collective-permute-start.33 = (bf16[2,256,1024]{2,1,0:T(8,128)(2,1)S(1)}, bf16[2,256,1024]{2,1,0:T(8,128)(2,1)S(1)}, u32[]{:S(2)}, u32[]{:S(2)}) collective-permute-start(bf16[2,256,1024]{2,1,0:T(8,128)(2,1)S(1)} %copy-done.12), channel_id=1, source_target_pairs={{4,0},{5,1},{6,2},{7,3},{8,4},{9,5},{10,6},{11,7},{12,8},{13,9},{1... | collective-permute-start | bytes 3145736 | tf_op jit(solution)/shard_map/ppermute | solution.py:210
  283.7 23.8 %collective-permute-start.40 = (bf16[2,16,1024]{2,1,0:T(8,128)(2,1)S(1)}, bf16[2,16,1024]{2,1,0:T(8,128)(2,1)S(1)}, u32[]{:S(2)}, u32[]{:S(2)}) collective-permute-start(bf16[2,16,1024]{2,1,0:T(8,128)(2,1)S(1)} %get-tuple-element.67), channel_id=1, source_target_pairs={{0,16},{1,17},{2,18},{3,19},{4,20},{5,21},{6,22},{7,23},{8,24},{9,... | collective-permute-start | bytes 196616 | tf_op jit(solution)/shard_map/ppermute | solution.py:210
  310.5 6.9 %collective-permute-start.29 = (bf16[2,256,1024]{2,1,0:T(8,128)(2,1)S(1)}, bf16[2,256,1024]{2,1,0:T(8,128)(2,1)S(1)}, u32[]{:S(2)}, u32[]{:S(2)}) collective-permute-start(bf16[2,256,1024]{2,1,0:T(8,128)(2,1)S(1)} %add_convert_fusion.4), channel_id=1, source_target_pairs={{4,0},{5,1},{6,2},{7,3},{8,4},{9,5},{10,6},{11,7},{12,8},{13,9},{1... | collective-permute-start | bytes 3145736 | tf_op jit(solution)/shard_map/ppermute | solution.py:210
  317.9 11.3 %collective-permute-start.41 = (bf16[2,16,1024]{2,1,0:T(8,128)(2,1)S(1)}, bf16[2,16,1024]{2,1,0:T(8,128)(2,1)S(1)}, u32[]{:S(2)}, u32[]{:S(2)}) collective-permute-start(bf16[2,16,1024]{2,1,0:T(8,128)(2,1)S(1)} %get-tuple-element.69), channel_id=1, source_target_pairs={{0,32},{1,33},{2,34},{3,35},{4,36},{5,37},{6,38},{7,39},{8,40},{9,... | collective-permute-start | bytes 196616 | tf_op jit(solution)/shard_map/ppermute | solution.py:210
  329.6 14.3 %collective-permute-start.32 = (bf16[2,256,1024]{2,1,0:T(8,128)(2,1)S(1)}, bf16[2,256,1024]{2,1,0:T(8,128)(2,1)S(1)}, u32[]{:S(2)}, u32[]{:S(2)}) collective-permute-start(bf16[2,256,1024]{2,1,0:T(8,128)(2,1)S(1)} %add_convert_fusion.2), channel_id=1, source_target_pairs={{0,4},{1,5},{2,6},{3,7},{4,8},{5,9},{6,10},{7,11},{8,12},{9,13},{1... | collective-permute-start | bytes 3145736 | tf_op jit(solution)/shard_map/ppermute | solution.py:210
  344.0 3.4 collective-permute-start.34
  347.7 18.1 %collective-permute-start.25 = (bf16[2,128,1024]{2,1,0:T(8,128)(2,1)S(1)}, bf16[2,128,1024]{2,1,0:T(8,128)(2,1)S(1)}, u32[]{:S(2)}, u32[]{:S(2)}) collective-permute-start(bf16[2,128,1024]{2,1,0:T(8,128)(2,1)S(1)} %get-tuple-element.55), channel_id=1, source_target_pairs={{0,3},{1,2},{2,1},{3,0},{4,7},{5,6},{6,5},{7,4},{8,11},{9,10},{10,... | collective-permute-start | bytes 1572872 | tf_op jit(solution)/shard_map/ppermute | solution.py:210
  365.8 87.4 %collective-permute-start.43 = (bf16[2,4,1024]{2,1,0:T(4,128)(2,1)S(1)}, bf16[2,4,1024]{2,1,0:T(4,128)(2,1)S(1)}, u32[]{:S(2)}, u32[]{:S(2)}) collective-permute-start(bf16[2,4,1024]{2,1,0:T(4,128)(2,1)S(1)} %get-tuple-element.70), channel_id=1, source_target_pairs={{0,4},{1,5},{2,6},{3,7},{4,0},{5,1},{6,2},{7,3},{8,12},{9,13},{10,... | collective-permute-start | bytes 49160 | tf_op jit(solution)/shard_map/ppermute | solution.py:210
  456.9 104.2 %collective-permute-start.24 = (bf16[2,128,1024]{2,1,0:T(8,128)(2,1)S(1)}, bf16[2,128,1024]{2,1,0:T(8,128)(2,1)S(1)}, u32[]{:S(2)}, u32[]{:S(2)}) collective-permute-start(bf16[2,128,1024]{2,1,0:T(8,128)(2,1)S(1)} %get-tuple-element.56), channel_id=1, source_target_pairs={{0,2},{1,3},{2,0},{3,1},{4,6},{5,7},{6,4},{7,5},{8,10},{9,11},{10,... | collective-permute-start | bytes 1572872 | tf_op jit(solution)/shard_map/ppermute | solution.py:210
  561.3 5.8 collective-permute-start.35
  567.8 5.4 collective-permute-done.24.refs_2_
  575.1 9.4 %collective-permute-done.36.refs_3_ = bf16[2,128,1024]{2,1,0:T(8,128)(2,1)S(1)} collective-permute-done((bf16[2,128,1024]{2,1,0:T(8,128)(2,1)S(1)}, bf16[2,128,1024]{2,1,0:T(8,128)(2,1)S(1)}, u32[]{:S(2)}, u32[]{:S(2)}) %collective-permute-start.36) | collective-permute-done | bytes 524320 | tf_op jit(solution)/shard_map/ppermute | solution.py:210
  584.4 6.3 %collective-permute-done.35.refs_2_ = bf16[2,128,1024]{2,1,0:T(8,128)(2,1)S(1)} collective-permute-done((bf16[2,128,1024]{2,1,0:T(8,128)(2,1)S(1)}, bf16[2,128,1024]{2,1,0:T(8,128)(2,1)S(1)}, u32[]{:S(2)}, u32[]{:S(2)}) %collective-permute-start.35) | collective-permute-done | bytes 524320 | tf_op jit(solution)/shard_map/ppermute | solution.py:210
  590.7 2.2 place.3
  (133 shorter events, 50.5 us)
Async XLA Ops:
  3.4 64.1 %collective-permute-start.3 = (bf16[2,128,1024]{2,1,0:T(8,128)(2,1)}, bf16[2,128,1024]{2,1,0:T(8,128)(2,1)S(1)}, u32[]{:S(2)}, u32[]{:S(2)}) collective-permute-start(bf16[2,128,1024]{2,1,0:T(8,128)(2,1)} %get-tuple-element.46), channel_id=1, source_target_pairs={{0,1},{1,0},{2,3},{3,2},{4,5},{5,4},{6,7},{7,6},{8,9},{9,8},{10,11... | collective-permute-start | bytes 1572872 | tf_op jit(solution)/shard_map/ppermute | solution.py:210
  3.4 69.7 %collective-permute-start.4 = (bf16[2,128,1024]{2,1,0:T(8,128)(2,1)}, bf16[2,128,1024]{2,1,0:T(8,128)(2,1)S(1)}, u32[]{:S(2)}, u32[]{:S(2)}) collective-permute-start(bf16[2,128,1024]{2,1,0:T(8,128)(2,1)} %get-tuple-element.45), channel_id=1, source_target_pairs={{0,2},{1,3},{2,0},{3,1},{4,6},{5,7},{6,4},{7,5},{8,10},{9,11},{10,... | collective-permute-start | bytes 1572872 | tf_op jit(solution)/shard_map/ppermute | solution.py:210
  13.8 61.8 %collective-permute-start.5 = (bf16[2,128,1024]{2,1,0:T(8,128)(2,1)}, bf16[2,128,1024]{2,1,0:T(8,128)(2,1)S(1)}, u32[]{:S(2)}, u32[]{:S(2)}) collective-permute-start(bf16[2,128,1024]{2,1,0:T(8,128)(2,1)} %get-tuple-element.44), channel_id=1, source_target_pairs={{0,3},{1,2},{2,1},{3,0},{4,7},{5,6},{6,5},{7,4},{8,11},{9,10},{10,... | collective-permute-start | bytes 1572872 | tf_op jit(solution)/shard_map/ppermute | solution.py:210
  16.6 44.0 %collective-permute-start.19 = (bf16[2,16,1024]{2,1,0:T(8,128)(2,1)S(1)}, bf16[2,16,1024]{2,1,0:T(8,128)(2,1)S(1)}, u32[]{:S(2)}, u32[]{:S(2)}) collective-permute-start(bf16[2,16,1024]{2,1,0:T(8,128)(2,1)S(1)} %pad_maximum_fusion.6), channel_id=1, source_target_pairs={{0,48},{1,49},{2,50},{3,51},{4,52},{5,53},{6,54},{7,55},{8,56},{9,... | collective-permute-start | bytes 196616 | tf_op jit(solution)/shard_map/ppermute | solution.py:210
  17.7 43.2 %collective-permute-start.18 = (bf16[2,16,1024]{2,1,0:T(8,128)(2,1)S(1)}, bf16[2,16,1024]{2,1,0:T(8,128)(2,1)S(1)}, u32[]{:S(2)}, u32[]{:S(2)}) collective-permute-start(bf16[2,16,1024]{2,1,0:T(8,128)(2,1)S(1)} %pad_maximum_fusion.6), channel_id=1, source_target_pairs={{0,32},{1,33},{2,34},{3,35},{4,36},{5,37},{6,38},{7,39},{8,40},{9,... | collective-permute-start | bytes 196616 | tf_op jit(solution)/shard_map/ppermute | solution.py:210
  69.6 49.4 %collective-permute-start.8 = (bf16[2,256,1024]{2,1,0:T(8,128)(2,1)S(1)}, bf16[2,256,1024]{2,1,0:T(8,128)(2,1)}, u32[]{:S(2)}, u32[]{:S(2)}) collective-permute-start(bf16[2,256,1024]{2,1,0:T(8,128)(2,1)S(1)} %pad_maximum_fusion.2.refs_2_), channel_id=1, source_target_pairs={{0,4},{1,5},{2,6},{3,7},{4,8},{5,9},{6,10},{7,11},{8,12},{9,13},{1... | collective-permute-start | bytes 3145736 | tf_op jit(solution)/shard_map/ppermute | solution.py:210
  73.1 47.8 %collective-permute-start.6 = (bf16[2,256,1024]{2,1,0:T(8,128)(2,1)S(1)}, bf16[2,256,1024]{2,1,0:T(8,128)(2,1)}, u32[]{:S(2)}, u32[]{:S(2)}) collective-permute-start(bf16[2,256,1024]{2,1,0:T(8,128)(2,1)S(1)} %pad_maximum_fusion.2.refs_2_), channel_id=1, source_target_pairs={{4,0},{5,1},{6,2},{7,3},{8,4},{9,5},{10,6},{11,7},{12,8},{13,9},{1... | collective-permute-start | bytes 3145736 | tf_op jit(solution)/shard_map/ppermute | solution.py:210
  75.7 75.5 %collective-permute-start.9 = (bf16[2,256,1024]{2,1,0:T(8,128)(2,1)S(1)}, bf16[2,256,1024]{2,1,0:T(8,128)(2,1)}, u32[]{:S(2)}, u32[]{:S(2)}) collective-permute-start(bf16[2,256,1024]{2,1,0:T(8,128)(2,1)S(1)} %constant_dynamic-update-slice_fusion.refs_3_), channel_id=1, source_target_pairs={{0,4},{1,5},{2,6},{3,7},{4,8},{5,9},{6,10},{7,11},{8,12},{9,13},{1... | collective-permute-start | bytes 3145736 | tf_op jit(solution)/shard_map/ppermute | solution.py:210
  79.1 74.0 %collective-permute-start.7 = (bf16[2,256,1024]{2,1,0:T(8,128)(2,1)S(1)}, bf16[2,256,1024]{2,1,0:T(8,128)(2,1)}, u32[]{:S(2)}, u32[]{:S(2)}) collective-permute-start(bf16[2,256,1024]{2,1,0:T(8,128)(2,1)S(1)} %constant_dynamic-update-slice_fusion.refs_3_), channel_id=1, source_target_pairs={{4,0},{5,1},{6,2},{7,3},{8,4},{9,5},{10,6},{11,7},{12,8},{13,9},{1... | collective-permute-start | bytes 3145736 | tf_op jit(solution)/shard_map/ppermute | solution.py:210
  115.3 44.0 %collective-permute-start.1 = (bf16[2,128,1024]{2,1,0:T(8,128)(2,1)S(1)}, bf16[2,128,1024]{2,1,0:T(8,128)(2,1)S(1)}, u32[]{:S(2)}, u32[]{:S(2)}) collective-permute-start(bf16[2,128,1024]{2,1,0:T(8,128)(2,1)S(1)} %pad_maximum_fusion.4), channel_id=1, source_target_pairs={{0,2},{1,3},{2,0},{3,1},{4,6},{5,7},{6,4},{7,5},{8,10},{9,11},{10,... | collective-permute-start | bytes 1572872 | tf_op jit(solution)/shard_map/ppermute | solution.py:210
  119.0 60.4 %collective-permute-start.12 = (bf16[2,256,1024]{2,1,0:T(8,128)(2,1)}, bf16[2,256,1024]{2,1,0:T(8,128)(2,1)}, u32[]{:S(2)}, u32[]{:S(2)}) collective-permute-start(bf16[2,256,1024]{2,1,0:T(8,128)(2,1)} %collective-permute-done.8.refs_6_), channel_id=1, source_target_pairs={{0,4},{1,5},{2,6},{3,7},{4,8},{5,9},{6,10},{7,11},{8,12},{9,13},{1... | collective-permute-start | bytes 3145736 | tf_op jit(solution)/shard_map/ppermute | solution.py:210
  120.9 58.5 %collective-permute-start.10 = (bf16[2,256,1024]{2,1,0:T(8,128)(2,1)}, bf16[2,256,1024]{2,1,0:T(8,128)(2,1)}, u32[]{:S(2)}, u32[]{:S(2)}) collective-permute-start(bf16[2,256,1024]{2,1,0:T(8,128)(2,1)} %collective-permute-done.6.refs_4_), channel_id=1, source_target_pairs={{4,0},{5,1},{6,2},{7,3},{8,4},{9,5},{10,6},{11,7},{12,8},{13,9},{1... | collective-permute-start | bytes 3145736 | tf_op jit(solution)/shard_map/ppermute | solution.py:210
  151.2 43.0 %collective-permute-start.13 = (bf16[2,256,1024]{2,1,0:T(8,128)(2,1)}, bf16[2,256,1024]{2,1,0:T(8,128)(2,1)}, u32[]{:S(2)}, u32[]{:S(2)}) collective-permute-start(bf16[2,256,1024]{2,1,0:T(8,128)(2,1)} %collective-permute-done.9.refs_7_), channel_id=1, source_target_pairs={{0,4},{1,5},{2,6},{3,7},{4,8},{5,9},{6,10},{7,11},{8,12},{9,13},{1... | collective-permute-start | bytes 3145736 | tf_op jit(solution)/shard_map/ppermute | solution.py:210
  153.2 42.8 %collective-permute-start.11 = (bf16[2,256,1024]{2,1,0:T(8,128)(2,1)}, bf16[2,256,1024]{2,1,0:T(8,128)(2,1)}, u32[]{:S(2)}, u32[]{:S(2)}) collective-permute-start(bf16[2,256,1024]{2,1,0:T(8,128)(2,1)} %collective-permute-done.7.refs_5_), channel_id=1, source_target_pairs={{4,0},{5,1},{6,2},{7,3},{8,4},{9,5},{10,6},{11,7},{12,8},{13,9},{1... | collective-permute-start | bytes 3145736 | tf_op jit(solution)/shard_map/ppermute | solution.py:210
  233.4 74.2 %collective-permute-start.26 = (bf16[2,256,1024]{2,1,0:T(8,128)(2,1)}, bf16[2,256,1024]{2,1,0:T(8,128)(2,1)S(1)}, u32[]{:S(2)}, u32[]{:S(2)}) collective-permute-start(bf16[2,256,1024]{2,1,0:T(8,128)(2,1)} %get-tuple-element.28), channel_id=1, source_target_pairs={{0,4},{1,5},{2,6},{3,7},{4,8},{5,9},{6,10},{7,11},{8,12},{9,13},{1... | collective-permute-start | bytes 3145736 | tf_op jit(solution)/shard_map/ppermute | solution.py:210
  237.9 35.1 %collective-permute-start.39 = (bf16[2,64,1024]{2,1,0:T(8,128)(2,1)S(1)}, bf16[2,64,1024]{2,1,0:T(8,128)(2,1)S(1)}, u32[]{:S(2)}, u32[]{:S(2)}) collective-permute-start(bf16[2,64,1024]{2,1,0:T(8,128)(2,1)S(1)} %get-tuple-element.49), channel_id=1, source_target_pairs={{0,192},{1,193},{2,194},{3,195},{4,196},{5,197},{6,198},{7,199},{8... | collective-permute-start | bytes 786440 | tf_op jit(solution)/shard_map/ppermute | solution.py:210
  239.3 43.3 %collective-permute-start.38 = (bf16[2,64,1024]{2,1,0:T(8,128)(2,1)S(1)}, bf16[2,64,1024]{2,1,0:T(8,128)(2,1)S(1)}, u32[]{:S(2)}, u32[]{:S(2)}) collective-permute-start(bf16[2,64,1024]{2,1,0:T(8,128)(2,1)S(1)} %get-tuple-element.50), channel_id=1, source_target_pairs={{0,128},{1,129},{2,130},{3,131},{4,132},{5,133},{6,134},{7,135},{8... | collective-permute-start | bytes 786440 | tf_op jit(solution)/shard_map/ppermute | solution.py:210
  240.8 67.2 %collective-permute-start.28 = (bf16[2,256,1024]{2,1,0:T(8,128)(2,1)}, bf16[2,256,1024]{2,1,0:T(8,128)(2,1)S(1)}, u32[]{:S(2)}, u32[]{:S(2)}) collective-permute-start(bf16[2,256,1024]{2,1,0:T(8,128)(2,1)} %get-tuple-element.30), channel_id=1, source_target_pairs={{4,0},{5,1},{6,2},{7,3},{8,4},{9,5},{10,6},{11,7},{12,8},{13,9},{1... | collective-permute-start | bytes 3145736 | tf_op jit(solution)/shard_map/ppermute | solution.py:210
  271.1 39.4 %collective-permute-start.31 = (bf16[2,256,1024]{2,1,0:T(8,128)(2,1)S(1)}, bf16[2,256,1024]{2,1,0:T(8,128)(2,1)S(1)}, u32[]{:S(2)}, u32[]{:S(2)}) collective-permute-start(bf16[2,256,1024]{2,1,0:T(8,128)(2,1)S(1)} %copy-done.13), channel_id=1, source_target_pairs={{0,4},{1,5},{2,6},{3,7},{4,8},{5,9},{6,10},{7,11},{8,12},{9,13},{1... | collective-permute-start | bytes 3145736 | tf_op jit(solution)/shard_map/ppermute | solution.py:210
  273.0 44.9 %collective-permute-start.33 = (bf16[2,256,1024]{2,1,0:T(8,128)(2,1)S(1)}, bf16[2,256,1024]{2,1,0:T(8,128)(2,1)S(1)}, u32[]{:S(2)}, u32[]{:S(2)}) collective-permute-start(bf16[2,256,1024]{2,1,0:T(8,128)(2,1)S(1)} %copy-done.12), channel_id=1, source_target_pairs={{4,0},{5,1},{6,2},{7,3},{8,4},{9,5},{10,6},{11,7},{12,8},{13,9},{1... | collective-permute-start | bytes 3145736 | tf_op jit(solution)/shard_map/ppermute | solution.py:210
  283.7 45.9 %collective-permute-start.40 = (bf16[2,16,1024]{2,1,0:T(8,128)(2,1)S(1)}, bf16[2,16,1024]{2,1,0:T(8,128)(2,1)S(1)}, u32[]{:S(2)}, u32[]{:S(2)}) collective-permute-start(bf16[2,16,1024]{2,1,0:T(8,128)(2,1)S(1)} %get-tuple-element.67), channel_id=1, source_target_pairs={{0,16},{1,17},{2,18},{3,19},{4,20},{5,21},{6,22},{7,23},{8,24},{9,... | collective-permute-start | bytes 196616 | tf_op jit(solution)/shard_map/ppermute | solution.py:210
  307.6 36.4 %collective-permute-start.42 = (bf16[2,16,1024]{2,1,0:T(8,128)(2,1)S(1)}, bf16[2,16,1024]{2,1,0:T(8,128)(2,1)S(1)}, u32[]{:S(2)}, u32[]{:S(2)}) collective-permute-start(bf16[2,16,1024]{2,1,0:T(8,128)(2,1)S(1)} %get-tuple-element.68), channel_id=1, source_target_pairs={{0,48},{1,49},{2,50},{3,51},{4,52},{5,53},{6,54},{7,55},{8,56},{9,... | collective-permute-start | bytes 196616 | tf_op jit(solution)/shard_map/ppermute | solution.py:210
  308.0 39.7 %collective-permute-start.27 = (bf16[2,256,1024]{2,1,0:T(8,128)(2,1)S(1)}, bf16[2,256,1024]{2,1,0:T(8,128)(2,1)S(1)}, u32[]{:S(2)}, u32[]{:S(2)}) collective-permute-start(bf16[2,256,1024]{2,1,0:T(8,128)(2,1)S(1)} %add_convert_fusion.5), channel_id=1, source_target_pairs={{0,4},{1,5},{2,6},{3,7},{4,8},{5,9},{6,10},{7,11},{8,12},{9,13},{1... | collective-permute-start | bytes 3145736 | tf_op jit(solution)/shard_map/ppermute | solution.py:210
  310.5 55.3 %collective-permute-start.29 = (bf16[2,256,1024]{2,1,0:T(8,128)(2,1)S(1)}, bf16[2,256,1024]{2,1,0:T(8,128)(2,1)S(1)}, u32[]{:S(2)}, u32[]{:S(2)}) collective-permute-start(bf16[2,256,1024]{2,1,0:T(8,128)(2,1)S(1)} %add_convert_fusion.4), channel_id=1, source_target_pairs={{4,0},{5,1},{6,2},{7,3},{8,4},{9,5},{10,6},{11,7},{12,8},{13,9},{1... | collective-permute-start | bytes 3145736 | tf_op jit(solution)/shard_map/ppermute | solution.py:210
  329.6 124.2 %collective-permute-start.32 = (bf16[2,256,1024]{2,1,0:T(8,128)(2,1)S(1)}, bf16[2,256,1024]{2,1,0:T(8,128)(2,1)S(1)}, u32[]{:S(2)}, u32[]{:S(2)}) collective-permute-start(bf16[2,256,1024]{2,1,0:T(8,128)(2,1)S(1)} %add_convert_fusion.2), channel_id=1, source_target_pairs={{0,4},{1,5},{2,6},{3,7},{4,8},{5,9},{6,10},{7,11},{8,12},{9,13},{1... | collective-permute-start | bytes 3145736 | tf_op jit(solution)/shard_map/ppermute | solution.py:210
  344.0 110.0 %collective-permute-start.34 = (bf16[2,256,1024]{2,1,0:T(8,128)(2,1)S(1)}, bf16[2,256,1024]{2,1,0:T(8,128)(2,1)S(1)}, u32[]{:S(2)}, u32[]{:S(2)}) collective-permute-start(bf16[2,256,1024]{2,1,0:T(8,128)(2,1)S(1)} %add_convert_fusion.1), channel_id=1, source_target_pairs={{4,0},{5,1},{6,2},{7,3},{8,4},{9,5},{10,6},{11,7},{12,8},{13,9},{1... | collective-permute-start | bytes 3145736 | tf_op jit(solution)/shard_map/ppermute | solution.py:210
  347.5 213.8 %collective-permute-start.23 = (bf16[2,128,1024]{2,1,0:T(8,128)(2,1)S(1)}, bf16[2,128,1024]{2,1,0:T(8,128)(2,1)S(1)}, u32[]{:S(2)}, u32[]{:S(2)}) collective-permute-start(bf16[2,128,1024]{2,1,0:T(8,128)(2,1)S(1)} %get-tuple-element.57), channel_id=1, source_target_pairs={{0,1},{1,0},{2,3},{3,2},{4,5},{5,4},{6,7},{7,6},{8,9},{9,8},{10,11... | collective-permute-start | bytes 1572872 | tf_op jit(solution)/shard_map/ppermute | solution.py:210
  347.7 220.1 %collective-permute-start.25 = (bf16[2,128,1024]{2,1,0:T(8,128)(2,1)S(1)}, bf16[2,128,1024]{2,1,0:T(8,128)(2,1)S(1)}, u32[]{:S(2)}, u32[]{:S(2)}) collective-permute-start(bf16[2,128,1024]{2,1,0:T(8,128)(2,1)S(1)} %get-tuple-element.55), channel_id=1, source_target_pairs={{0,3},{1,2},{2,1},{3,0},{4,7},{5,6},{6,5},{7,4},{8,11},{9,10},{10,... | collective-permute-start | bytes 1572872 | tf_op jit(solution)/shard_map/ppermute | solution.py:210
  365.8 91.1 %collective-permute-start.43 = (bf16[2,4,1024]{2,1,0:T(4,128)(2,1)S(1)}, bf16[2,4,1024]{2,1,0:T(4,128)(2,1)S(1)}, u32[]{:S(2)}, u32[]{:S(2)}) collective-permute-start(bf16[2,4,1024]{2,1,0:T(4,128)(2,1)S(1)} %get-tuple-element.70), channel_id=1, source_target_pairs={{0,4},{1,5},{2,6},{3,7},{4,0},{5,1},{6,2},{7,3},{8,12},{9,13},{10,... | collective-permute-start | bytes 49160 | tf_op jit(solution)/shard_map/ppermute | solution.py:210
  453.9 107.2 %collective-permute-start.45 = (bf16[2,4,1024]{2,1,0:T(4,128)(2,1)S(1)}, bf16[2,4,1024]{2,1,0:T(4,128)(2,1)S(1)}, u32[]{:S(2)}, u32[]{:S(2)}) collective-permute-start(bf16[2,4,1024]{2,1,0:T(4,128)(2,1)S(1)} %get-tuple-element.71), channel_id=1, source_target_pairs={{0,12},{1,13},{2,14},{3,15},{4,8},{5,9},{6,10},{7,11},{8,4},{9,5},... | collective-permute-start | bytes 49160 | tf_op jit(solution)/shard_map/ppermute | solution.py:210
  454.0 107.1 %collective-permute-start.44 = (bf16[2,4,1024]{2,1,0:T(4,128)(2,1)S(1)}, bf16[2,4,1024]{2,1,0:T(4,128)(2,1)S(1)}, u32[]{:S(2)}, u32[]{:S(2)}) collective-permute-start(bf16[2,4,1024]{2,1,0:T(4,128)(2,1)S(1)} %get-tuple-element.72), channel_id=1, source_target_pairs={{0,8},{1,9},{2,10},{3,11},{4,12},{5,13},{6,14},{7,15},{8,0},{9,1},... | collective-permute-start | bytes 49160 | tf_op jit(solution)/shard_map/ppermute | solution.py:210
  456.9 116.3 %collective-permute-start.24 = (bf16[2,128,1024]{2,1,0:T(8,128)(2,1)S(1)}, bf16[2,128,1024]{2,1,0:T(8,128)(2,1)S(1)}, u32[]{:S(2)}, u32[]{:S(2)}) collective-permute-start(bf16[2,128,1024]{2,1,0:T(8,128)(2,1)S(1)} %get-tuple-element.56), channel_id=1, source_target_pairs={{0,2},{1,3},{2,0},{3,1},{4,6},{5,7},{6,4},{7,5},{8,10},{9,11},{10,... | collective-permute-start | bytes 1572872 | tf_op jit(solution)/shard_map/ppermute | solution.py:210
  (31 other events, 675.4 us)

commit v2 on v1

v2 whole, which is shorter than its diff:
```python
import math

import jax
import jax.numpy as jnp
from jax import lax
from jax.experimental import pallas as pl
from jax.experimental.pallas import tpu as pltpu
from jax.sharding import Mesh, PartitionSpec as P

HD = 128
SOURCES = 6
MASKED_SCORE = -1e30
ROOT = HD ** (-0.5)
LOG2E = math.log2(math.e)
F32 = jnp.float32
BF16 = jnp.bfloat16


def nt(a, b):
    return lax.dot_general(a, b, (((1,), (1,)), ((), ())), preferred_element_type=F32)


def nn(a, b):
    return lax.dot_general(a, b, (((1,), (0,)), ((), ())), preferred_element_type=F32)


def tn(a, b):
    return lax.dot_general(a, b, (((0,), (0,)), ((), ())), preferred_element_type=F32)


def fold8(op, x):
    return op(x.reshape(x.shape[0] // 8, 8, x.shape[1]), axis=0)


def load_rows(qg, q_s, g_s, gt_s):
    half = qg[0].shape[1]
    for h in range(2):
        q_s[h * half : (h + 1) * half] = qg[h][0]
        g_s[h * half : (h + 1) * half] = qg[h][1]
    gt_s[...] = g_s[...].astype(F32).T


def text_kernel(text_len, qg0, qg1, text, out_terms, out_rows, out_dq, q_s, g_s, gt_s):
    load_rows((qg0, qg1), q_s, g_s, gt_s)
    parts, _, part_rows, _ = text.shape
    keys = text[:, 0].reshape(parts * part_rows, HD)
    values = text[:, 1].reshape(parts * part_rows, HD)
    row = lax.broadcasted_iota(jnp.int32, (parts * part_rows, 1), 0)
    s = jnp.where(row < text_len[0], nt(keys, q_s[...]), MASKED_SCORE)
    e = jnp.exp2((s - jnp.max(s, axis=0, keepdims=True)) * (ROOT * LOG2E))
    p = (e * (1.0 / jnp.sum(e, axis=0, keepdims=True))).astype(BF16)
    rows = tn(values, p)
    dot = jnp.sum(rows * gt_s[...], axis=0, keepdims=True)
    ds = (p.astype(F32) * (nt(values, g_s[...]) - dot)).astype(BF16)
    out_rows[...] = rows
    out_dq[...] = tn(keys, ds)
    out_terms[:, 0] = (nn(ds, q_s[...]) * ROOT).astype(BF16).reshape(parts, part_rows, HD)
    out_terms[:, 1] = nn(p, g_s[...]).astype(BF16).reshape(parts, part_rows, HD)


def text_attention(text_len, qg, text):
    half, width = qg[0].shape[1:]
    heads = width // HD
    rows = 2 * half
    tile = pl.BlockSpec((2, half, HD), lambda h, n: (0, 0, h))
    text_tile = pl.BlockSpec((*text.shape[:3], HD), lambda h, n: (0, 0, 0, h))
    turned = pl.BlockSpec((HD, rows), lambda h, n: (h, 0))
    text_rows = text.shape[0] * text.shape[2]
    return pl.pallas_call(
        text_kernel,
        grid_spec=pltpu.PrefetchScalarGridSpec(
            num_scalar_prefetch=1,
            grid=(heads,),
            in_specs=[tile, tile, text_tile],
            out_specs=[text_tile, turned, turned],
            scratch_shapes=[
                pltpu.VMEM((rows, HD), BF16),
                pltpu.VMEM((rows, HD), BF16),
                pltpu.VMEM((HD, rows), F32),
            ],
        ),
        out_shape=[
            jax.ShapeDtypeStruct(text.shape, BF16),
            jax.ShapeDtypeStruct((width, rows), F32),
            jax.ShapeDtypeStruct((width, rows), F32),
        ],
        compiler_params=pltpu.CompilerParams(vmem_limit_bytes=32 * 2**20),
        cost_estimate=pl.CostEstimate(
            flops=12 * heads * rows * text_rows * HD,
            bytes_accessed=16 * half * width,
            transcendentals=heads * rows * text_rows,
        ),
        name="text_attention",
    )(text_len, *qg, text)


def attention_kernel(meta, *refs):
    n = SOURCES
    qg = refs[0:2]
    kv = [refs[2 + 2 * i : 4 + 2 * i] for i in range(n)]
    text_rows, text_dq = refs[2 + 2 * n : 4 + 2 * n]
    outs = refs[4 + 2 * n :]
    out_q = outs[0:2]
    out_kv = [outs[2 + 2 * i : 4 + 2 * i] for i in range(n)]
    q_s, g_s, gt_s, s_s, p_s, top_s, sum_s, acc_s = outs[2 + 2 * n :]
    half = qg[0].shape[1]
    scale2 = ROOT * LOG2E
    load_rows(qg, q_s, g_s, gt_s)
    acc_s[1] = text_dq[...]

    def scores(i):
        for h in range(2):
            s = nt(kv[i][h][0], q_s[...])
            s_s[i, h * half : (h + 1) * half] = s
            top = fold8(jnp.max, s)
            if i == 0 and h == 0:
                top_s[...] = top
            else:
                top_s[...] = jnp.maximum(top_s[...], top)

    def exps(i):
        top = jnp.max(top_s[...], axis=0, keepdims=True)
        for h in range(2):
            e = jnp.exp2((s_s[i, h * half : (h + 1) * half] - top) * scale2)
            s_s[i, h * half : (h + 1) * half] = e
            part = fold8(jnp.sum, e)
            if i == 0 and h == 0:
                sum_s[...] = part
            else:
                sum_s[...] += part

    def values(i):
        inverse = 1.0 / jnp.sum(sum_s[...], axis=0, keepdims=True)
        for h in range(2):
            p = (s_s[i, h * half : (h + 1) * half] * inverse).astype(BF16)
            p_s[i, h * half : (h + 1) * half] = p
            o = tn(kv[i][h][1], p)
            if i == 0 and h == 0:
                acc_s[0] = o
            else:
                acc_s[0] += o
            out_kv[i][h][1] = nn(p, g_s[...]).astype(BF16)

    def grads(i):
        dot = top_s[0:1]
        for h in range(2):
            dp = nt(kv[i][h][1], g_s[...])
            p = p_s[i, h * half : (h + 1) * half].astype(F32)
            ds = (p * (dp - dot)).astype(BF16)
            out_kv[i][h][0] = (nn(ds, q_s[...]) * ROOT).astype(BF16)
            acc_s[1] += tn(kv[i][h][0], ds)

    def each(step):
        step(0)
        for i in range(1, n):
            pl.when(meta[i] > 0)(lambda i=i: step(i))

    each(scores)
    each(exps)
    each(values)
    self_out = acc_s[0]
    top_s[0:1] = jnp.sum(self_out * gt_s[...], axis=0, keepdims=True)
    rows_out = (self_out + text_rows[...]).T.astype(BF16)
    each(grads)
    for i in range(1, n):

        @pl.when(meta[i] == 0)
        def _():
            for h in range(2):
                out_kv[i][h][...] = jnp.zeros_like(out_kv[i][h])

    rows_dq = (acc_s[1] * ROOT).T.astype(BF16)
    for h in range(2):
        out_q[h][0] = rows_out[h * half : (h + 1) * half]
        out_q[h][1] = rows_dq[h * half : (h + 1) * half]


def attention(meta, qg, kv, text_rows, text_dq):
    half, width = qg[0].shape[1:]
    heads = width // HD
    rows = 2 * half
    n = SOURCES
    tile = pl.BlockSpec((2, half, HD), lambda h, meta: (0, 0, h))
    turned = pl.BlockSpec((HD, rows), lambda h, meta: (h, 0))
    part = jax.ShapeDtypeStruct((2, half, width), BF16)
    keys = 3 * rows
    return pl.pallas_call(
        attention_kernel,
        grid_spec=pltpu.PrefetchScalarGridSpec(
            num_scalar_prefetch=1,
            grid=(heads,),
            in_specs=[tile] * (2 + 2 * n) + [turned, turned],
            out_specs=[tile] * (2 + 2 * n),
            scratch_shapes=[
                pltpu.VMEM((rows, HD), BF16),
                pltpu.VMEM((rows, HD), BF16),
                pltpu.VMEM((HD, rows), F32),
                pltpu.VMEM((n, rows, rows), F32),
                pltpu.VMEM((n, rows, rows), BF16),
                pltpu.VMEM((8, rows), F32),
                pltpu.VMEM((8, rows), F32),
                pltpu.VMEM((2, HD, rows), F32),
            ],
        ),
        out_shape=[part] * (2 + 2 * n),
        compiler_params=pltpu.CompilerParams(vmem_limit_bytes=48 * 2**20),
        cost_estimate=pl.CostEstimate(
            flops=12 * heads * rows * keys * HD,
            bytes_accessed=2 * (4 + 4 * n) * half * width * 2,
            transcendentals=heads * rows * keys,
        ),
        name="attention",
    )(meta, *qg, *[part for pair in kv for part in pair], text_rows, text_dq)


def place_kernel(meta, *refs):
    pieces = refs[0:4]
    outs = refs[4:]
    width = pieces[0].shape[2]
    for m in range(4):
        start = pl.multiple_of((meta[0] ^ m) * width, width)
        for i, out in enumerate(outs):
            out[:, pl.ds(start, width)] = pieces[m][i].astype(out.dtype)


def place(enc, pieces, dtypes):
    _, rows, width = pieces[0].shape
    return pl.pallas_call(
        place_kernel,
        in_specs=[pl.BlockSpec(memory_space=pltpu.SMEM)] + [pl.BlockSpec(memory_space=pltpu.VMEM)] * 4,
        out_specs=[pl.BlockSpec(memory_space=pltpu.VMEM)] * len(dtypes),
        out_shape=[jax.ShapeDtypeStruct((rows, 4 * width), d) for d in dtypes],
        compiler_params=pltpu.CompilerParams(vmem_limit_bytes=24 * 2**20),
        cost_estimate=pl.CostEstimate(flops=0, bytes_accessed=rows * width * 4 * 12, transcendentals=0),
        name="place",
    )(enc, *pieces)


CTX = ("y", "z_lo", "x")
ENC = ("z_hi", "core")
SIZES = {"y": 4, "z_lo": 4, "x": 4, "z_hi": 2, "core": 2}


def shards(qkv, grad_out, text_kv, text_len, key_tiles, key_count):
    ctx_size, enc_size = lax.axis_size(CTX), lax.axis_size(ENC)
    ctx, enc = lax.axis_index(CTX), lax.axis_index(ENC)
    width = qkv.shape[2] // enc_size
    rows = qkv.shape[1]
    plane = ("z_lo", "x")
    row_len = lax.axis_size("x")
    lane = lax.axis_index("x")
    even = lane % 2 == 0

    def send(block, target):
        route = []
        for c in range(ctx_size):
            for e in range(enc_size):
                to = target(c, e)
                if 0 <= to[0] < ctx_size:
                    route.append((c * enc_size + e, to[0] * enc_size + to[1]))
        return lax.ppermute(block, CTX + ENC, route)

    def swap(block, m):
        return send(block, lambda c, e: (c, e ^ m))

    def rotate(block, d):
        return send(block, lambda c, e: (c - c % row_len + (c + d) % row_len, e))

    def pair(block):
        return send(block, lambda c, e: (c ^ 1, e))

    def next_row(block, sign):
        return send(block, lambda c, e: (c + sign * (row_len if c % row_len < 2 else -row_len), e))

    def columns(block, m):
        return lax.dynamic_slice_in_dim(block, (enc ^ m) * width, width, block.ndim - 1)

    def tie(blocks, done):
        return lax.optimization_barrier((blocks, done))

    text = text_kv.reshape(1, -1, width)
    text = jnp.broadcast_to(text, (lax.axis_size(plane), *text.shape[1:]))
    text = lax.all_to_all(text, plane, split_axis=0, concat_axis=0, tiled=True)
    text = text.reshape(-1, *text_kv.shape).transpose(1, 0, 2, 3).reshape(2, -1, width)

    kv_own = [columns(qkv[1:3], m) for m in range(4)]
    kv_in = [swap(kv_own[m], m) if m else kv_own[m] for m in range(4)]
    own = [jnp.concatenate(kv_in[0:2], 1), None]
    left, right, far, across, paired = ([None, None] for _ in range(5))
    qg_in = [None] * 4

    def qg_columns(q, g, m):
        return jnp.stack([columns(q, m), columns(g, m)])

    left[0], right[0] = rotate(own[0], 1), rotate(own[0], -1)
    across[0] = next_row(jnp.where(even, left[0], right[0]), 1)
    far[0] = rotate(left[0], 1)
    q_g = (qkv[0], grad_out)
    (kv_in[2:4], q_g), (left[0], right[0], far[0], text) = tie(
        (kv_in[2:4], q_g), (left[0], right[0], far[0], text)
    )
    text = lax.all_gather(text, "y", axis=0)

    own[1] = jnp.concatenate(kv_in[2:4], 1)
    qg_in[3] = swap(qg_columns(*q_g, 3), 3)
    qg_in[1] = swap(qg_columns(*q_g, 1), 1)
    left[1], right[1] = rotate(own[1], 1), rotate(own[1], -1)
    (left[1], right[1], across[0]), (qg_in[3], q_g) = tie((left[1], right[1], across[0]), (qg_in[3], q_g))

    across[1] = next_row(jnp.where(even, left[1], right[1]), 1)
    qg_in[2] = swap(qg_columns(*q_g, 2), 2)
    far[1] = rotate(right[1], -1)
    paired[0] = pair(across[0])
    across[1], (qg_in[2], far[1], paired[0], text) = tie(across[1], (qg_in[2], far[1], paired[0], text))

    paired[1] = pair(across[1])
    qg_in[0] = qg_columns(*q_g, 0)
    qg = [jnp.concatenate(qg_in[0:2], 1), jnp.concatenate(qg_in[2:4], 1)]
    grad_text, text_rows, text_dq = text_attention(text_len, qg, text)
    paired[1], (grad_text, text_rows, text_dq) = tie(paired[1], (grad_text, text_rows, text_dq))
    grad_text = lax.psum_scatter(grad_text, "y", scatter_dimension=0)

    my_tiles = lax.dynamic_index_in_dim(key_tiles, ctx, 0, keepdims=False)
    my_count = lax.dynamic_index_in_dim(key_count, ctx, 0, keepdims=False)
    listed = jnp.arange(my_tiles.shape[0]) < my_count
    row = ctx - lane
    outer = (lane == 0) | (lane == row_len - 1)
    side = jnp.where(lane < 2, -1, 1)
    sources = jnp.stack(
        [
            ctx,
            row + (lane + row_len - 1) % row_len,
            row + (lane + 1) % row_len,
            row + (lane + 2) % row_len,
            ctx + 2 * side,
            jnp.where(outer, ctx + side, -1),
        ]
    )
    used = (my_tiles[None, :] == sources[:, None]) & listed[None, :]
    meta = jnp.sum(used, axis=1).astype(jnp.int32)

    outs = attention(meta, qg, [own, left, right, far, paired, across], text_rows, text_dq)
    out_q = outs[0:2]
    terms = [list(outs[2 + 2 * i : 4 + 2 * i]) for i in range(SOURCES)]
    t_own, t_left, t_right, t_far, t_paired, t_across = terms

    def piece(halves, m):
        return halves[m // 2][:, (m % 2) * rows : (m % 2 + 1) * rows]

    def add(*blocks):
        return sum(b.astype(F32) for b in blocks).astype(BF16)

    back_q = [piece(out_q, m) for m in range(4)]
    met, relayed, crossed, to_right, to_left, grad_halves = ([None, None] for _ in range(6))

    back_q[1], back_q[2] = swap(back_q[1], 1), swap(back_q[2], 2)
    met[1] = pair(t_paired[1])
    met[1], (back_q[2], back_q[3], t_far[1], t_paired[0], grad_text) = tie(
        met[1], (back_q[2], back_q[3], t_far[1], t_paired[0], grad_text)
    )
    grad_text = grad_text.reshape(2, -1, text_kv.shape[1], width).transpose(1, 0, 2, 3)
    grad_text = grad_text.reshape(-1, 2 * text_kv.shape[1], width)
    grad_text = lax.all_to_all(grad_text, plane, split_axis=0, concat_axis=0, tiled=True)

    crossed[1] = next_row(add(t_across[1], met[1]), -1)
    back_q[3] = swap(back_q[3], 3)
    relayed[1] = rotate(t_far[1], 1)
    met[0] = pair(t_paired[0])
    (crossed[1], relayed[1]), (met[0], back_q[3], t_far[0], grad_text) = tie(
        (crossed[1], relayed[1]), (met[0], back_q[3], t_far[0], grad_text)
    )

    def totals(h):
        none = jnp.zeros_like(crossed[h])
        to_right = add(t_right[h], jnp.where(even, none, crossed[h]), *([relayed[h]] if h else []))
        to_left = add(t_left[h], jnp.where(even, crossed[h], none), *([] if h else [relayed[h]]))
        return rotate(to_right, 1), rotate(to_left, -1)

    last = totals(1)
    crossed[0] = next_row(add(t_across[0], met[0]), -1)
    relayed[0] = rotate(t_far[0], -1)
    last, (crossed[0], relayed[0]) = tie(last, (crossed[0], relayed[0]))
    grad_halves[1] = add(t_own[1], *last)
    grad_halves[0] = add(t_own[0], *totals(0))
    back_kv = [piece(grad_halves, m) for m in range(4)]
    back_kv[1:4] = [swap(back_kv[m], m) for m in (1, 2, 3)]

    grad_text = jnp.sum(grad_text.astype(F32), axis=0).reshape(text_kv.shape)

    meta_enc = enc.astype(jnp.int32).reshape(1)
    attn_out, grad_q = place(meta_enc, back_q, (BF16, F32))
    grad_k, grad_v = place(meta_enc, back_kv, (F32, F32))
    return (attn_out, grad_q, grad_k, grad_v, grad_text)


def solution(mesh):
    fine = Mesh(mesh.devices.reshape(tuple(SIZES.values())), tuple(SIZES))
    tokens = P(CTX + ENC, None)
    in_specs = (P(None, CTX + ENC, None), tokens, P(None, CTX, ENC), P(), P(), P())
    out_specs = (tokens, tokens, tokens, tokens, P(None, CTX, ENC))
    return jax.shard_map(shards, mesh=fine, in_specs=in_specs, out_specs=out_specs, check_vma=False)
```

time: 587 us -> 477 us (0.81); the launches traced: 593 us -> 469 us
  starting transfers between devices: 404 us -> 108 us
  waiting for transfers between devices: 116 us -> 207 us
  blocking collectives: 0 us -> 50.6 us
  between operations: 5.31 us -> 15.2 us
  local copies, waits for them, and re-layouts: 13.3 us -> 22.8 us
  Pallas kernels: 41.5 us -> 48.6 us
    ppermute x46 -> x32, starting transfers between devices: 404 us -> 99.8 us  [send(): return lax.ppermute(block, CTX + ENC, route)]
    ppermute x46 -> x32, waiting for transfers between devices: 116 us -> 194 us  [send(): return lax.ppermute(block, CTX + ENC, route)]
    all_to_all x0 -> x1, blocking collectives: none -> 50.6 us  [shards(): lax.all_to_all(grad_text, plane, split_axis=0, concat_axis=0, tiled=True)]
    all_to_all x0 -> x1, waiting for transfers between devices: none -> 13.8 us  [shards(): text = lax.all_to_all(text, plane, split_axis=0, concat_axis=0, tiled=True)]
    pallas_call x0 -> x1, Pallas kernels: none -> 9 us  [text_attention(): pl.pallas_call(text_kernel, grid_spec=pltpu.PrefetchScalarGridSpec(num_sc...]
    all_to_all x0 -> x1, starting transfers between devices: none -> 8.45 us  [shards(): text = lax.all_to_all(text, plane, split_axis=0, concat_axis=0, tiled=True)]
  transfers between devices with their start and end apart: 46 -> 35, of which waited for: 11 -> 15; matrix products, arithmetic and copies ran while one was open for 4% -> 5% of each run, Pallas kernels for 0% -> 10%
where the time goes in v2:
time: 477 us; the launch traced here: 469 us
  waiting for transfers between devices  207 us (43%)
  starting transfers between devices  108 us (23%)
  blocking collectives  50.6 us (11%)
  Pallas kernels  48.6 us (10%)
  local copies, waits for them, and re-layouts  22.8 us (5%)
  other arithmetic  16.1 us (3%)
  between operations  15.2 us (3%)
    ppermute x32, waiting for transfers between devices, send(): return lax.ppermute(block, CTX + ENC, route)  194 us
    ppermute x32, starting transfers between devices, send(): return lax.ppermute(block, CTX + ENC, route)  99.8 us
    all_to_all x1, blocking collectives, shards(): lax.all_to_all(grad_text, plane, split_axis=0, concat_axis=0, tiled=True)  50.6 us
    pallas_call x1, Pallas kernels, attention(): pl.pallas_call(attention_kernel, grid_spec=pltpu.PrefetchScalarGridSpec(n...  33.1 us
    all_to_all x1, waiting for transfers between devices, shards(): text = lax.all_to_all(text, plane, split_axis=0, concat_axis=0, tiled=True)  13.8 us
  transfers between devices with their start and end apart: 35, of which 15 were waited for; matrix products, arithmetic and copies ran while one was open for 5% of the time, Pallas kernels for 10%

profile of v2, /device:TPU:42, one launch (start us, length us, event | category | flops | bytes accessed | tf_op | source)
XLA Modules:
  0.0 469.1 jit_solution(11747877406227496247)
XLA Ops:
  14.8 8.5 %all-to-all-start = ((bf16[16,8,1024]{2,1,0:T(8,128)(2,1)}), bf16[16,8,1024]{2,1,0:T(8,128)(2,1)S(1)}, u32[]{:S(2)}, u32[]{:S(2)}) async-start(bf16[16,8,1024]{2,1,0:T(8,128)(2,1)} %broadcast_in_dim.5), calls=%async_computation | async-start | bytes 524288 | tf_op jit(solution)/shard_map/all_to_all | solution.py:283
  23.3 3.2 collective-permute-start.1
  28.0 11.7 %collective-permute-done.3.refs_4_ = bf16[2,256,1024]{2,1,0:T(8,128)(2,1)S(1)} collective-permute-done((bf16[2,256,1024]{2,1,0:T(8,128)(2,1)S(1)}, bf16[2,256,1024]{2,1,0:T(8,128)(2,1)S(1)}, u32[]{:S(2)}, u32[]{:S(2)}) %collective-permute-start.3) | collective-permute-done | bytes 1048608 | tf_op jit(solution)/shard_map/ppermute | solution.py:261
  42.5 13.8 %all-to-all-done = bf16[16,8,1024]{2,1,0:T(8,128)(2,1)S(1)} async-done(((bf16[16,8,1024]{2,1,0:T(8,128)(2,1)}), bf16[16,8,1024]{2,1,0:T(8,128)(2,1)S(1)}, u32[]{:S(2)}, u32[]{:S(2)}) %all-to-all-start) | async-done | bytes 262176 | tf_op jit(solution)/shard_map/all_to_all | solution.py:283
  59.1 4.2 collective-permute-start.8
  63.3 11.7 %collective-permute-done = bf16[2,128,1024]{2,1,0:T(8,128)(2,1)} collective-permute-done((bf16[2,128,1024]{2,1,0:T(8,128)(2,1)}, bf16[2,128,1024]{2,1,0:T(8,128)(2,1)}, u32[]{:S(2)}, u32[]{:S(2)}) %collective-permute-start) | collective-permute-done | bytes 524320 | tf_op jit(solution)/shard_map/ppermute | solution.py:261
  78.7 35.7 %collective-permute-start.7 = (bf16[2,256,1024]{2,1,0:T(8,128)(2,1)}, bf16[2,256,1024]{2,1,0:T(8,128)(2,1)S(1)}, u32[]{:S(2)}, u32[]{:S(2)}) collective-permute-start(bf16[2,256,1024]{2,1,0:T(8,128)(2,1)} %constant_dynamic-update-slice_fusion.refs_3_), channel_id=1, source_target_pairs={{0,12},{1,13},{2,14},{3,15},{4,0},{5,1},{6,2},{7,3},{8,4},{9,5},{1... | collective-permute-start | bytes 3145736 | tf_op jit(solution)/shard_map/ppermute | solution.py:261
  116.9 22.1 %collective-permute-done.9 = bf16[2,128,1024]{2,1,0:T(8,128)(2,1)} collective-permute-done((bf16[2,128,1024]{2,1,0:T(8,128)(2,1)}, bf16[2,128,1024]{2,1,0:T(8,128)(2,1)}, u32[]{:S(2)}, u32[]{:S(2)}) %collective-permute-start.9) | collective-permute-done | bytes 524320 | tf_op jit(solution)/shard_map/ppermute | solution.py:261
  140.2 2.6 collective-permute-start.11
  142.8 3.1 collective-permute-start.14
  146.9 3.8 collective-permute-start.12
  150.9 43.8 %collective-permute-done.12 = bf16[2,128,1024]{2,1,0:T(8,128)(2,1)S(1)} collective-permute-done((bf16[2,128,1024]{2,1,0:T(8,128)(2,1)S(1)}, bf16[2,128,1024]{2,1,0:T(8,128)(2,1)S(1)}, u32[]{:S(2)}, u32[]{:S(2)}) %collective-permute-start.12) | collective-permute-done | bytes 524320 | tf_op jit(solution)/shard_map/ppermute | solution.py:261
  194.7 4.8 %collective-permute-start.15 = (bf16[2,256,1024]{2,1,0:T(8,128)(2,1)}, bf16[2,256,1024]{2,1,0:T(8,128)(2,1)S(1)}, u32[]{:S(2)}, u32[]{:S(2)}) collective-permute-start(bf16[2,256,1024]{2,1,0:T(8,128)(2,1)} %collective-permute-done.11.refs_13_), channel_id=1, source_target_pairs={{0,4},{1,5},{2,6},{3,7},{4,0},{5,1},{6,2},{7,3},{8,12},{9,13},{10,... | collective-permute-start | bytes 3145736 | tf_op jit(solution)/shard_map/ppermute | solution.py:261
  203.6 9.0 %text_attention.1 = (bf16[4,2,64,1024]{3,2,1,0:T(8,128)(2,1)}, f32[1024,512]{1,0:T(8,128)S(1)}, f32[1024,512]{1,0:T(8,128)S(1)}) custom-call(s32[1]{0:T(128)S(6)} %copy.27.text_len, bf16[2,256,1024]{2,1,0:T(8,128)(2,1)S(1)} %pad_maximum_fusion.1.qg0.refs_0_, bf16[2,256,1024]{2,1,0:T(8,128)(2,1)S(1)} %constant_dynamic-update-slice_fusion.2.qg1.refs_1_, ...), custom_call_target="tpu_custom_call" | custom-call | flops 1610612736 | bytes 4194304 | tf_op jit(solution)/shard_map/text_attention/pallas_call | solution.py:69
  215.2 7.9 %collective-permute-done.15.refs_11_ = bf16[2,256,1024]{2,1,0:T(8,128)(2,1)S(1)} collective-permute-done((bf16[2,256,1024]{2,1,0:T(8,128)(2,1)}, bf16[2,256,1024]{2,1,0:T(8,128)(2,1)S(1)}, u32[]{:S(2)}, u32[]{:S(2)}) %collective-permute-start.15) | collective-permute-done | bytes 1048608 | tf_op jit(solution)/shard_map/ppermute | solution.py:261
  224.2 33.1 %attention.1 = (bf16[2,256,1024]{2,1,0:T(8,128)(2,1)S(1)}, bf16[2,256,1024]{2,1,0:T(8,128)(2,1)S(1)}, bf16[2,256,1024]{2,1,0:T(8,128)(2,1)S(1)}, bf16[2,256,1024...) custom-call(s32[6]{0:T(128)S(1)} %convert_reduce_fusion.1.meta, ...), custom_call_target="tpu_custom_call" | custom-call | flops 9663676416 | bytes 29360128 | tf_op jit(solution)/shard_map/attention/pallas_call | solution.py:187
  257.4 13.5 %collective-permute-start.17 = (bf16[2,256,1024]{2,1,0:T(8,128)(2,1)}, bf16[2,256,1024]{2,1,0:T(8,128)(2,1)}, u32[]{:S(2)}, u32[]{:S(2)}) collective-permute-start(bf16[2,256,1024]{2,1,0:T(8,128)(2,1)} %get-tuple-element.91), channel_id=1, source_target_pairs={{0,4},{1,5},{2,6},{3,7},{4,0},{5,1},{6,2},{7,3},{8,12},{9,13},{10,... | collective-permute-start | bytes 3145736 | tf_op jit(solution)/shard_map/ppermute | solution.py:261
  271.8 4.6 collective-permute-start.18
  276.4 19.8 %collective-permute-done.18.refs_2_ = bf16[2,128,1024]{2,1,0:T(8,128)(2,1)S(1)} collective-permute-done((bf16[2,128,1024]{2,1,0:T(8,128)(2,1)S(1)}, bf16[2,128,1024]{2,1,0:T(8,128)(2,1)S(1)}, u32[]{:S(2)}, u32[]{:S(2)}) %collective-permute-start.18) | collective-permute-done | bytes 524320 | tf_op jit(solution)/shard_map/ppermute | solution.py:261
  296.9 2.9 add_convert_fusion.7
  305.6 50.6 %all_to_all.10 = bf16[16,8,1024]{2,1,0:T(8,128)(2,1)S(1)} all-to-all(bf16[16,8,1024]{2,1,0:T(8,128)(2,1)S(1)} %copy.24), channel_id=1, replica_groups=mesh['y'=4,'z_lo'=4,'x'=4,'z_hi'=2,'core'=2] {'z_lo','x'}, dimensions={0} | all-to-all | bytes 524288 | tf_op jit(solution)/shard_map/all_to_all | solution.py:363
  356.3 2.8 add_convert_fusion.5
  362.7 3.0 collective-permute-start.25
  367.2 18.0 %collective-permute-done.24 = bf16[2,256,1024]{2,1,0:T(8,128)(2,1)S(1)} collective-permute-done((bf16[2,256,1024]{2,1,0:T(8,128)(2,1)S(1)}, bf16[2,256,1024]{2,1,0:T(8,128)(2,1)S(1)}, u32[]{:S(2)}, u32[]{:S(2)}) %collective-permute-start.24) | collective-permute-done | bytes 1048608 | tf_op jit(solution)/shard_map/ppermute | solution.py:261
  387.7 17.6 %collective-permute-done.26 = bf16[2,256,1024]{2,1,0:T(8,128)(2,1)S(1)} collective-permute-done((bf16[2,256,1024]{2,1,0:T(8,128)(2,1)S(1)}, bf16[2,256,1024]{2,1,0:T(8,128)(2,1)S(1)}, u32[]{:S(2)}, u32[]{:S(2)}) %collective-permute-start.26) | collective-permute-done | bytes 1048608 | tf_op jit(solution)/shard_map/ppermute | solution.py:261
  411.9 5.1 %collective-permute-start.30 = (bf16[2,128,1024]{2,1,0:T(8,128)(2,1)S(1)}, bf16[2,128,1024]{2,1,0:T(8,128)(2,1)}, u32[]{:S(2)}, u32[]{:S(2)}) collective-permute-start(bf16[2,128,1024]{2,1,0:T(8,128)(2,1)S(1)} %get-tuple-element.130), channel_id=1, source_target_pairs={{0,2},{1,3},{2,0},{3,1},{4,6},{5,7},{6,4},{7,5},{8,10},{9,11},{10,... | collective-permute-start | bytes 1572872 | tf_op jit(solution)/shard_map/ppermute | solution.py:261
  416.9 12.3 %collective-permute-done.27 = bf16[2,256,1024]{2,1,0:T(8,128)(2,1)S(1)} collective-permute-done((bf16[2,256,1024]{2,1,0:T(8,128)(2,1)S(1)}, bf16[2,256,1024]{2,1,0:T(8,128)(2,1)S(1)}, u32[]{:S(2)}, u32[]{:S(2)}) %collective-permute-start.27) | collective-permute-done | bytes 1048608 | tf_op jit(solution)/shard_map/ppermute | solution.py:261
  429.2 2.8 collective-permute-done.28
  434.2 3.0 place.2
  437.3 10.2 %collective-permute-done.31.refs_3_ = bf16[2,128,1024]{2,1,0:T(8,128)(2,1)} collective-permute-done((bf16[2,128,1024]{2,1,0:T(8,128)(2,1)}, bf16[2,128,1024]{2,1,0:T(8,128)(2,1)}, u32[]{:S(2)}, u32[]{:S(2)}) %collective-permute-start.31) | collective-permute-done | bytes 524320 | tf_op jit(solution)/shard_map/ppermute | solution.py:261
  447.5 11.3 %collective-permute-done.30.refs_2_ = bf16[2,128,1024]{2,1,0:T(8,128)(2,1)} collective-permute-done((bf16[2,128,1024]{2,1,0:T(8,128)(2,1)S(1)}, bf16[2,128,1024]{2,1,0:T(8,128)(2,1)}, u32[]{:S(2)}, u32[]{:S(2)}) %collective-permute-start.30) | collective-permute-done | bytes 524320 | tf_op jit(solution)/shard_map/ppermute | solution.py:261
  458.8 3.4 place.3
  (142 shorter events, 54.1 us)
Async XLA Ops:
  12.0 27.7 %collective-permute-start.3 = (bf16[2,256,1024]{2,1,0:T(8,128)(2,1)S(1)}, bf16[2,256,1024]{2,1,0:T(8,128)(2,1)S(1)}, u32[]{:S(2)}, u32[]{:S(2)}) collective-permute-start(bf16[2,256,1024]{2,1,0:T(8,128)(2,1)S(1)} %pad_maximum_fusion.refs_2_), channel_id=1, source_target_pairs={{0,4},{1,5},{2,6},{3,7},{4,8},{5,9},{6,10},{7,11},{8,12},{9,13},{1... | collective-permute-start | bytes 3145736 | tf_op jit(solution)/shard_map/ppermute | solution.py:261
  13.6 43.2 %collective-permute-start.4 = (bf16[2,256,1024]{2,1,0:T(8,128)(2,1)S(1)}, bf16[2,256,1024]{2,1,0:T(8,128)(2,1)}, u32[]{:S(2)}, u32[]{:S(2)}) collective-permute-start(bf16[2,256,1024]{2,1,0:T(8,128)(2,1)S(1)} %pad_maximum_fusion.refs_2_), channel_id=1, source_target_pairs={{0,12},{1,13},{2,14},{3,15},{4,0},{5,1},{6,2},{7,3},{8,4},{9,5},{1... | collective-permute-start | bytes 3145736 | tf_op jit(solution)/shard_map/ppermute | solution.py:261
  14.8 41.5 %all-to-all-start = ((bf16[16,8,1024]{2,1,0:T(8,128)(2,1)}), bf16[16,8,1024]{2,1,0:T(8,128)(2,1)S(1)}, u32[]{:S(2)}, u32[]{:S(2)}) async-start(bf16[16,8,1024]{2,1,0:T(8,128)(2,1)} %broadcast_in_dim.5), calls=%async_computation | async-start | bytes 524288 | tf_op jit(solution)/shard_map/all_to_all | solution.py:283
  23.3 127.6 %all-gather.3.cloned.1.call-start = ((), (), s32[]{:S(2)}) async-start(), calls=%async_computation.4 | async-start | bytes 1310720 | tf_op jit(solution)/shard_map/all_gather | solution.py:302
  23.3 39.9 %collective-permute-start.1 = (bf16[2,128,1024]{2,1,0:T(8,128)(2,1)}, bf16[2,128,1024]{2,1,0:T(8,128)(2,1)}, u32[]{:S(2)}, u32[]{:S(2)}) collective-permute-start(bf16[2,128,1024]{2,1,0:T(8,128)(2,1)} %get-tuple-element.127), channel_id=1, source_target_pairs={{0,3},{1,2},{2,1},{3,0},{4,7},{5,6},{6,5},{7,4},{8,11},{9,10},{10,... | collective-permute-start | bytes 1572872 | tf_op jit(solution)/shard_map/ppermute | solution.py:261
  26.5 48.4 %collective-permute-start = (bf16[2,128,1024]{2,1,0:T(8,128)(2,1)}, bf16[2,128,1024]{2,1,0:T(8,128)(2,1)}, u32[]{:S(2)}, u32[]{:S(2)}) collective-permute-start(bf16[2,128,1024]{2,1,0:T(8,128)(2,1)} %get-tuple-element.128), channel_id=1, source_target_pairs={{0,2},{1,3},{2,0},{3,1},{4,6},{5,7},{6,4},{7,5},{8,10},{9,11},{10,... | collective-permute-start | bytes 1572872 | tf_op jit(solution)/shard_map/ppermute | solution.py:261
  39.7 35.2 %collective-permute-start.5 = (bf16[2,256,1024]{2,1,0:T(8,128)(2,1)S(1)}, bf16[2,256,1024]{2,1,0:T(8,128)(2,1)}, u32[]{:S(2)}, u32[]{:S(2)}) collective-permute-start(bf16[2,256,1024]{2,1,0:T(8,128)(2,1)S(1)} %collective-permute-done.3.refs_4_), channel_id=1, source_target_pairs={{0,4},{1,5},{2,6},{3,7},{4,8},{5,9},{6,10},{7,11},{8,12},{9,13},{1... | collective-permute-start | bytes 3145736 | tf_op jit(solution)/shard_map/ppermute | solution.py:261
  59.1 57.8 %collective-permute-start.8 = (bf16[2,256,1024]{2,1,0:T(8,128)(2,1)}, bf16[2,256,1024]{2,1,0:T(8,128)(2,1)}, u32[]{:S(2)}, u32[]{:S(2)}) collective-permute-start(bf16[2,256,1024]{2,1,0:T(8,128)(2,1)} %broadcast_select_fusion.1), channel_id=1, source_target_pairs={{0,16},{1,17},{2,18},{3,19},{4,20},{5,21},{6,22},{7,23},{16,32},{1... | collective-permute-start | bytes 3145736 | tf_op jit(solution)/shard_map/ppermute | solution.py:261
  78.7 60.3 %collective-permute-start.7 = (bf16[2,256,1024]{2,1,0:T(8,128)(2,1)}, bf16[2,256,1024]{2,1,0:T(8,128)(2,1)S(1)}, u32[]{:S(2)}, u32[]{:S(2)}) collective-permute-start(bf16[2,256,1024]{2,1,0:T(8,128)(2,1)} %constant_dynamic-update-slice_fusion.refs_3_), channel_id=1, source_target_pairs={{0,12},{1,13},{2,14},{3,15},{4,0},{5,1},{6,2},{7,3},{8,4},{9,5},{1... | collective-permute-start | bytes 3145736 | tf_op jit(solution)/shard_map/ppermute | solution.py:261
  114.4 24.6 %collective-permute-start.6 = (bf16[2,256,1024]{2,1,0:T(8,128)(2,1)}, bf16[2,256,1024]{2,1,0:T(8,128)(2,1)S(1)}, u32[]{:S(2)}, u32[]{:S(2)}) collective-permute-start(bf16[2,256,1024]{2,1,0:T(8,128)(2,1)} %constant_dynamic-update-slice_fusion.refs_3_), channel_id=1, source_target_pairs={{0,4},{1,5},{2,6},{3,7},{4,8},{5,9},{6,10},{7,11},{8,12},{9,13},{1... | collective-permute-start | bytes 3145736 | tf_op jit(solution)/shard_map/ppermute | solution.py:261
  116.8 180.1 %reduce-scatter.2.cloned.1.call-start = ((), (), s32[]{:S(2)}) async-start(), calls=%async_computation.3 | async-start | bytes 1310720 | tf_op jit(solution)/shard_map/reduce_scatter | solution.py:321
  140.2 54.5 %collective-permute-start.11 = (bf16[2,256,1024]{2,1,0:T(8,128)(2,1)}, bf16[2,256,1024]{2,1,0:T(8,128)(2,1)}, u32[]{:S(2)}, u32[]{:S(2)}) collective-permute-start(bf16[2,256,1024]{2,1,0:T(8,128)(2,1)} %broadcast_select_fusion), channel_id=1, source_target_pairs={{0,16},{1,17},{2,18},{3,19},{4,20},{5,21},{6,22},{7,23},{16,32},{1... | collective-permute-start | bytes 3145736 | tf_op jit(solution)/shard_map/ppermute | solution.py:261
  142.8 51.9 %collective-permute-start.14 = (bf16[2,256,1024]{2,1,0:T(8,128)(2,1)}, bf16[2,256,1024]{2,1,0:T(8,128)(2,1)}, u32[]{:S(2)}, u32[]{:S(2)}) collective-permute-start(bf16[2,256,1024]{2,1,0:T(8,128)(2,1)} %collective-permute-done.8.refs_12_), channel_id=1, source_target_pairs={{0,4},{1,5},{2,6},{3,7},{4,0},{5,1},{6,2},{7,3},{8,12},{9,13},{10,... | collective-permute-start | bytes 3145736 | tf_op jit(solution)/shard_map/ppermute | solution.py:261
  145.9 48.8 %collective-permute-start.13 = (bf16[2,256,1024]{2,1,0:T(8,128)(2,1)S(1)}, bf16[2,256,1024]{2,1,0:T(8,128)(2,1)}, u32[]{:S(2)}, u32[]{:S(2)}) collective-permute-start(bf16[2,256,1024]{2,1,0:T(8,128)(2,1)S(1)} %collective-permute-done.7.refs_7_), channel_id=1, source_target_pairs={{0,12},{1,13},{2,14},{3,15},{4,0},{5,1},{6,2},{7,3},{8,4},{9,5},{1... | collective-permute-start | bytes 3145736 | tf_op jit(solution)/shard_map/ppermute | solution.py:261
  146.9 47.8 %collective-permute-start.12 = (bf16[2,128,1024]{2,1,0:T(8,128)(2,1)S(1)}, bf16[2,128,1024]{2,1,0:T(8,128)(2,1)S(1)}, u32[]{:S(2)}, u32[]{:S(2)}) collective-permute-start(bf16[2,128,1024]{2,1,0:T(8,128)(2,1)S(1)} %pad_maximum_fusion.4), channel_id=1, source_target_pairs={{0,2},{1,3},{2,0},{3,1},{4,6},{5,7},{6,4},{7,5},{8,10},{9,11},{10,... | collective-permute-start | bytes 1572872 | tf_op jit(solution)/shard_map/ppermute | solution.py:261
  150.8 49.9 %collective-permute-start.10 = (bf16[2,128,1024]{2,1,0:T(8,128)(2,1)S(1)}, bf16[2,128,1024]{2,1,0:T(8,128)(2,1)}, u32[]{:S(2)}, u32[]{:S(2)}) collective-permute-start(bf16[2,128,1024]{2,1,0:T(8,128)(2,1)S(1)} %pad_maximum_fusion.3), channel_id=1, source_target_pairs={{0,1},{1,0},{2,3},{3,2},{4,5},{5,4},{6,7},{7,6},{8,9},{9,8},{10,11... | collective-permute-start | bytes 1572872 | tf_op jit(solution)/shard_map/ppermute | solution.py:261
  194.7 28.4 %collective-permute-start.15 = (bf16[2,256,1024]{2,1,0:T(8,128)(2,1)}, bf16[2,256,1024]{2,1,0:T(8,128)(2,1)S(1)}, u32[]{:S(2)}, u32[]{:S(2)}) collective-permute-start(bf16[2,256,1024]{2,1,0:T(8,128)(2,1)} %collective-permute-done.11.refs_13_), channel_id=1, source_target_pairs={{0,4},{1,5},{2,6},{3,7},{4,0},{5,1},{6,2},{7,3},{8,12},{9,13},{10,... | collective-permute-start | bytes 3145736 | tf_op jit(solution)/shard_map/ppermute | solution.py:261
  257.4 39.5 %collective-permute-start.17 = (bf16[2,256,1024]{2,1,0:T(8,128)(2,1)}, bf16[2,256,1024]{2,1,0:T(8,128)(2,1)}, u32[]{:S(2)}, u32[]{:S(2)}) collective-permute-start(bf16[2,256,1024]{2,1,0:T(8,128)(2,1)} %get-tuple-element.91), channel_id=1, source_target_pairs={{0,4},{1,5},{2,6},{3,7},{4,0},{5,1},{6,2},{7,3},{8,12},{9,13},{10,... | collective-permute-start | bytes 3145736 | tf_op jit(solution)/shard_map/ppermute | solution.py:261
  271.8 24.3 %collective-permute-start.18 = (bf16[2,128,1024]{2,1,0:T(8,128)(2,1)S(1)}, bf16[2,128,1024]{2,1,0:T(8,128)(2,1)S(1)}, u32[]{:S(2)}, u32[]{:S(2)}) collective-permute-start(bf16[2,128,1024]{2,1,0:T(8,128)(2,1)S(1)} %get-tuple-element.138), channel_id=1, source_target_pairs={{0,2},{1,3},{2,0},{3,1},{4,6},{5,7},{6,4},{7,5},{8,10},{9,11},{10,... | collective-permute-start | bytes 1572872 | tf_op jit(solution)/shard_map/ppermute | solution.py:261
  299.9 56.4 %collective-permute-start.19 = (bf16[2,256,1024]{2,1,0:T(8,128)(2,1)}, bf16[2,256,1024]{2,1,0:T(8,128)(2,1)}, u32[]{:S(2)}, u32[]{:S(2)}) collective-permute-start(bf16[2,256,1024]{2,1,0:T(8,128)(2,1)} %add_convert_fusion.7), channel_id=1, source_target_pairs={{8,24},{9,25},{10,26},{11,27},{12,28},{13,29},{14,30},{15,31},{16,... | collective-permute-start | bytes 3145736 | tf_op jit(solution)/shard_map/ppermute | solution.py:261
  301.8 54.5 %collective-permute-start.20 = (bf16[2,256,1024]{2,1,0:T(8,128)(2,1)}, bf16[2,256,1024]{2,1,0:T(8,128)(2,1)}, u32[]{:S(2)}, u32[]{:S(2)}) collective-permute-start(bf16[2,256,1024]{2,1,0:T(8,128)(2,1)} %get-tuple-element.99), channel_id=1, source_target_pairs={{0,4},{1,5},{2,6},{3,7},{4,8},{5,9},{6,10},{7,11},{8,12},{9,13},{1... | collective-permute-start | bytes 3145736 | tf_op jit(solution)/shard_map/ppermute | solution.py:261
  301.9 54.4 %collective-permute-start.21 = (bf16[2,256,1024]{2,1,0:T(8,128)(2,1)}, bf16[2,256,1024]{2,1,0:T(8,128)(2,1)}, u32[]{:S(2)}, u32[]{:S(2)}) collective-permute-start(bf16[2,256,1024]{2,1,0:T(8,128)(2,1)} %get-tuple-element.100), channel_id=1, source_target_pairs={{0,4},{1,5},{2,6},{3,7},{4,0},{5,1},{6,2},{7,3},{8,12},{9,13},{10,... | collective-permute-start | bytes 3145736 | tf_op jit(solution)/shard_map/ppermute | solution.py:261
  303.9 52.3 %collective-permute-start.22 = (bf16[2,128,1024]{2,1,0:T(8,128)(2,1)}, bf16[2,128,1024]{2,1,0:T(8,128)(2,1)}, u32[]{:S(2)}, u32[]{:S(2)}) collective-permute-start(bf16[2,128,1024]{2,1,0:T(8,128)(2,1)} %get-tuple-element.101), channel_id=1, source_target_pairs={{0,3},{1,2},{2,1},{3,0},{4,7},{5,6},{6,5},{7,4},{8,11},{9,10},{10,... | collective-permute-start | bytes 1572872 | tf_op jit(solution)/shard_map/ppermute | solution.py:261
  359.0 26.2 %collective-permute-start.24 = (bf16[2,256,1024]{2,1,0:T(8,128)(2,1)S(1)}, bf16[2,256,1024]{2,1,0:T(8,128)(2,1)S(1)}, u32[]{:S(2)}, u32[]{:S(2)}) collective-permute-start(bf16[2,256,1024]{2,1,0:T(8,128)(2,1)S(1)} %get-tuple-element.135), channel_id=1, source_target_pairs={{0,12},{1,13},{2,14},{3,15},{4,0},{5,1},{6,2},{7,3},{8,4},{9,5},{1... | collective-permute-start | bytes 3145736 | tf_op jit(solution)/shard_map/ppermute | solution.py:261
  359.3 25.9 %collective-permute-start.23 = (bf16[2,256,1024]{2,1,0:T(8,128)(2,1)S(1)}, bf16[2,256,1024]{2,1,0:T(8,128)(2,1)S(1)}, u32[]{:S(2)}, u32[]{:S(2)}) collective-permute-start(bf16[2,256,1024]{2,1,0:T(8,128)(2,1)S(1)} %get-tuple-element.136), channel_id=1, source_target_pairs={{0,4},{1,5},{2,6},{3,7},{4,8},{5,9},{6,10},{7,11},{8,12},{9,13},{1... | collective-permute-start | bytes 3145736 | tf_op jit(solution)/shard_map/ppermute | solution.py:261
  362.7 25.0 %collective-permute-start.25 = (bf16[2,256,1024]{2,1,0:T(8,128)(2,1)S(1)}, bf16[2,256,1024]{2,1,0:T(8,128)(2,1)S(1)}, u32[]{:S(2)}, u32[]{:S(2)}) collective-permute-start(bf16[2,256,1024]{2,1,0:T(8,128)(2,1)S(1)} %add_convert_fusion.4), channel_id=1, source_target_pairs={{8,24},{9,25},{10,26},{11,27},{12,28},{13,29},{14,30},{15,31},{16,... | collective-permute-start | bytes 3145736 | tf_op jit(solution)/shard_map/ppermute | solution.py:261
  365.7 39.6 %collective-permute-start.26 = (bf16[2,256,1024]{2,1,0:T(8,128)(2,1)S(1)}, bf16[2,256,1024]{2,1,0:T(8,128)(2,1)S(1)}, u32[]{:S(2)}, u32[]{:S(2)}) collective-permute-start(bf16[2,256,1024]{2,1,0:T(8,128)(2,1)S(1)} %copy-done.25), channel_id=1, source_target_pairs={{0,12},{1,13},{2,14},{3,15},{4,0},{5,1},{6,2},{7,3},{8,4},{9,5},{1... | collective-permute-start | bytes 3145736 | tf_op jit(solution)/shard_map/ppermute | solution.py:261
  407.9 24.1 %collective-permute-start.28 = (bf16[2,256,1024]{2,1,0:T(8,128)(2,1)S(1)}, bf16[2,256,1024]{2,1,0:T(8,128)(2,1)S(1)}, u32[]{:S(2)}, u32[]{:S(2)}) collective-permute-start(bf16[2,256,1024]{2,1,0:T(8,128)(2,1)S(1)} %get-tuple-element.134), channel_id=1, source_target_pairs={{0,12},{1,13},{2,14},{3,15},{4,0},{5,1},{6,2},{7,3},{8,4},{9,5},{1... | collective-permute-start | bytes 3145736 | tf_op jit(solution)/shard_map/ppermute | solution.py:261
  409.3 24.9 %collective-permute-start.16 = (bf16[2,128,1024]{2,1,0:T(8,128)(2,1)}, bf16[2,128,1024]{2,1,0:T(8,128)(2,1)}, u32[]{:S(2)}, u32[]{:S(2)}) collective-permute-start(bf16[2,128,1024]{2,1,0:T(8,128)(2,1)} %get-tuple-element.139), channel_id=1, source_target_pairs={{0,1},{1,0},{2,3},{3,2},{4,5},{5,4},{6,7},{7,6},{8,9},{9,8},{10,11... | collective-permute-start | bytes 1572872 | tf_op jit(solution)/shard_map/ppermute | solution.py:261
  410.9 36.6 %collective-permute-start.31 = (bf16[2,128,1024]{2,1,0:T(8,128)(2,1)}, bf16[2,128,1024]{2,1,0:T(8,128)(2,1)}, u32[]{:S(2)}, u32[]{:S(2)}) collective-permute-start(bf16[2,128,1024]{2,1,0:T(8,128)(2,1)} %get-tuple-element.129), channel_id=1, source_target_pairs={{0,3},{1,2},{2,1},{3,0},{4,7},{5,6},{6,5},{7,4},{8,11},{9,10},{10,... | collective-permute-start | bytes 1572872 | tf_op jit(solution)/shard_map/ppermute | solution.py:261
  411.9 46.9 %collective-permute-start.30 = (bf16[2,128,1024]{2,1,0:T(8,128)(2,1)S(1)}, bf16[2,128,1024]{2,1,0:T(8,128)(2,1)}, u32[]{:S(2)}, u32[]{:S(2)}) collective-permute-start(bf16[2,128,1024]{2,1,0:T(8,128)(2,1)S(1)} %get-tuple-element.130), channel_id=1, source_target_pairs={{0,2},{1,3},{2,0},{3,1},{4,6},{5,7},{6,4},{7,5},{8,10},{9,11},{10,... | collective-permute-start | bytes 1572872 | tf_op jit(solution)/shard_map/ppermute | solution.py:261
  433.5 25.2 %collective-permute-start.29 = (bf16[2,128,1024]{2,1,0:T(8,128)(2,1)}, bf16[2,128,1024]{2,1,0:T(8,128)(2,1)S(1)}, u32[]{:S(2)}, u32[]{:S(2)}) collective-permute-start(bf16[2,128,1024]{2,1,0:T(8,128)(2,1)} %get-tuple-element.131), channel_id=1, source_target_pairs={{0,1},{1,0},{2,3},{3,2},{4,5},{5,4},{6,7},{7,6},{8,9},{9,8},{10,11... | collective-permute-start | bytes 1572872 | tf_op jit(solution)/shard_map/ppermute | solution.py:261
  (31 other events, 797.5 us)
Sparse Core Ops, SparseCore 0:
  117.0 32.4 all-gather.2
  223.3 26.2 reduce-scatter.1

commit v3 on v2

--- a/solution.py
+++ b/solution.py
@@ -366,8 +366,8 @@
     back_q[3] = swap(back_q[3], 3)
     relayed[1] = rotate(t_far[1], 1)
     met[0] = pair(t_paired[0])
-    (crossed[1], relayed[1]), (met[0], back_q[3], t_far[0], grad_text) = tie(
-        (crossed[1], relayed[1]), (met[0], back_q[3], t_far[0], grad_text)
+    (crossed[1], relayed[1]), (met[0], back_q[3], t_far[0]) = tie(
+        (crossed[1], relayed[1]), (met[0], back_q[3], t_far[0])
     )
 
     def totals(h):
@@ -379,7 +379,7 @@
     last = totals(1)
     crossed[0] = next_row(add(t_across[0], met[0]), -1)
     relayed[0] = rotate(t_far[0], -1)
-    last, (crossed[0], relayed[0]) = tie(last, (crossed[0], relayed[0]))
+    last, (crossed[0], relayed[0], grad_text) = tie(last, (crossed[0], relayed[0], grad_text))
     grad_halves[1] = add(t_own[1], *last)
     grad_halves[0] = add(t_own[0], *totals(0))
     back_kv = [piece(grad_halves, m) for m in range(4)]

time: 477 us -> 470 us (0.985)
  blocking collectives: 50.6 us -> 42.6 us
    all_to_all x1, blocking collectives: 50.6 us -> 42.6 us  [shards(): lax.all_to_all(grad_text, plane, split_axis=0, concat_axis=0, tiled=True)]
  transfers between devices with their start and end apart: 35 -> 35, of which waited for: 15 -> 14; matrix products, arithmetic and copies ran while one was open for 5% -> 5% of each run, Pallas kernels for 10% -> 10%
where the time goes in v3:
time: 470 us; the launch traced here: 462 us
  waiting for transfers between devices  209 us (44%)
  starting transfers between devices  109 us (23%)
  Pallas kernels  46.3 us (10%)
  blocking collectives  42.6 us (9%)
  local copies, waits for them, and re-layouts  22.2 us (5%)
  other arithmetic  17.5 us (4%)
  between operations  15.3 us (3%)
    ppermute x32, waiting for transfers between devices, send(): return lax.ppermute(block, CTX + ENC, route)  195 us
    ppermute x32, starting transfers between devices, send(): return lax.ppermute(block, CTX + ENC, route)  101 us
    all_to_all x1, blocking collectives, shards(): lax.all_to_all(grad_text, plane, split_axis=0, concat_axis=0, tiled=True)  42.6 us
    pallas_call x1, Pallas kernels, attention(): pl.pallas_call(attention_kernel, grid_spec=pltpu.PrefetchScalarGridSpec(n...  33.1 us
    all_to_all x1, waiting for transfers between devices, shards(): text = lax.all_to_all(text, plane, split_axis=0, concat_axis=0, tiled=True)  13.8 us
    convert_element_type x6, other arithmetic, add(): return sum((b.astype(F32) for b in blocks)).astype(BF16)  10.9 us
  transfers between devices with their start and end apart: 35, of which 14 were waited for; matrix products, arithmetic and copies ran while one was open for 5% of the time, Pallas kernels for 10%

profile of v3, /device:TPU:42, one launch (start us, length us, event | category | flops | bytes accessed | tf_op | source)
XLA Modules:
  0.0 461.9 jit_solution(17401154896456604577)
XLA Ops:
  14.8 8.5 %all-to-all-start = ((bf16[16,8,1024]{2,1,0:T(8,128)(2,1)}), bf16[16,8,1024]{2,1,0:T(8,128)(2,1)S(1)}, u32[]{:S(2)}, u32[]{:S(2)}) async-start(bf16[16,8,1024]{2,1,0:T(8,128)(2,1)} %broadcast_in_dim.5), calls=%async_computation | async-start | bytes 524288 | tf_op jit(solution)/shard_map/all_to_all | solution.py:283
  23.3 3.2 collective-permute-start.1
  28.0 11.7 %collective-permute-done.3.refs_4_ = bf16[2,256,1024]{2,1,0:T(8,128)(2,1)S(1)} collective-permute-done((bf16[2,256,1024]{2,1,0:T(8,128)(2,1)S(1)}, bf16[2,256,1024]{2,1,0:T(8,128)(2,1)S(1)}, u32[]{:S(2)}, u32[]{:S(2)}) %collective-permute-start.3) | collective-permute-done | bytes 1048608 | tf_op jit(solution)/shard_map/ppermute | solution.py:261
  42.5 13.8 %all-to-all-done = bf16[16,8,1024]{2,1,0:T(8,128)(2,1)S(1)} async-done(((bf16[16,8,1024]{2,1,0:T(8,128)(2,1)}), bf16[16,8,1024]{2,1,0:T(8,128)(2,1)S(1)}, u32[]{:S(2)}, u32[]{:S(2)}) %all-to-all-start) | async-done | bytes 262176 | tf_op jit(solution)/shard_map/all_to_all | solution.py:283
  56.7 2.3 broadcast_select_fusion.1
  59.1 4.2 collective-permute-start.8
  63.3 11.7 %collective-permute-done = bf16[2,128,1024]{2,1,0:T(8,128)(2,1)} collective-permute-done((bf16[2,128,1024]{2,1,0:T(8,128)(2,1)}, bf16[2,128,1024]{2,1,0:T(8,128)(2,1)}, u32[]{:S(2)}, u32[]{:S(2)}) %collective-permute-start) | collective-permute-done | bytes 524320 | tf_op jit(solution)/shard_map/ppermute | solution.py:261
  78.7 35.7 %collective-permute-start.7 = (bf16[2,256,1024]{2,1,0:T(8,128)(2,1)}, bf16[2,256,1024]{2,1,0:T(8,128)(2,1)S(1)}, u32[]{:S(2)}, u32[]{:S(2)}) collective-permute-start(bf16[2,256,1024]{2,1,0:T(8,128)(2,1)} %constant_dynamic-update-slice_fusion.refs_3_), channel_id=1, source_target_pairs={{0,12},{1,13},{2,14},{3,15},{4,0},{5,1},{6,2},{7,3},{8,4},{9,5},{1... | collective-permute-start | bytes 3145736 | tf_op jit(solution)/shard_map/ppermute | solution.py:261
  116.9 22.1 %collective-permute-done.9 = bf16[2,128,1024]{2,1,0:T(8,128)(2,1)} collective-permute-done((bf16[2,128,1024]{2,1,0:T(8,128)(2,1)}, bf16[2,128,1024]{2,1,0:T(8,128)(2,1)}, u32[]{:S(2)}, u32[]{:S(2)}) %collective-permute-start.9) | collective-permute-done | bytes 524320 | tf_op jit(solution)/shard_map/ppermute | solution.py:261
  140.2 2.6 collective-permute-start.11
  142.9 3.0 collective-permute-start.14
  147.0 3.8 collective-permute-start.12
  150.9 43.8 %collective-permute-done.12 = bf16[2,128,1024]{2,1,0:T(8,128)(2,1)S(1)} collective-permute-done((bf16[2,128,1024]{2,1,0:T(8,128)(2,1)S(1)}, bf16[2,128,1024]{2,1,0:T(8,128)(2,1)S(1)}, u32[]{:S(2)}, u32[]{:S(2)}) %collective-permute-start.12) | collective-permute-done | bytes 524320 | tf_op jit(solution)/shard_map/ppermute | solution.py:261
  194.7 4.8 %collective-permute-start.15 = (bf16[2,256,1024]{2,1,0:T(8,128)(2,1)}, bf16[2,256,1024]{2,1,0:T(8,128)(2,1)S(1)}, u32[]{:S(2)}, u32[]{:S(2)}) collective-permute-start(bf16[2,256,1024]{2,1,0:T(8,128)(2,1)} %collective-permute-done.11.refs_13_), channel_id=1, source_target_pairs={{0,4},{1,5},{2,6},{3,7},{4,0},{5,1},{6,2},{7,3},{8,12},{9,13},{10,... | collective-permute-start | bytes 3145736 | tf_op jit(solution)/shard_map/ppermute | solution.py:261
  203.6 9.0 %text_attention.1 = (bf16[4,2,64,1024]{3,2,1,0:T(8,128)(2,1)}, f32[1024,512]{1,0:T(8,128)S(1)}, f32[1024,512]{1,0:T(8,128)S(1)}) custom-call(s32[1]{0:T(128)S(6)} %copy.27.text_len, bf16[2,256,1024]{2,1,0:T(8,128)(2,1)S(1)} %pad_maximum_fusion.1.qg0.refs_0_, bf16[2,256,1024]{2,1,0:T(8,128)(2,1)S(1)} %constant_dynamic-update-slice_fusion.2.qg1.refs_1_, ...), custom_call_target="tpu_custom_call" | custom-call | flops 1610612736 | bytes 4194304 | tf_op jit(solution)/shard_map/text_attention/pallas_call | solution.py:69
  215.3 7.9 %collective-permute-done.15.refs_11_ = bf16[2,256,1024]{2,1,0:T(8,128)(2,1)S(1)} collective-permute-done((bf16[2,256,1024]{2,1,0:T(8,128)(2,1)}, bf16[2,256,1024]{2,1,0:T(8,128)(2,1)S(1)}, u32[]{:S(2)}, u32[]{:S(2)}) %collective-permute-start.15) | collective-permute-done | bytes 1048608 | tf_op jit(solution)/shard_map/ppermute | solution.py:261
  224.3 33.1 %attention.1 = (bf16[2,256,1024]{2,1,0:T(8,128)(2,1)S(1)}, bf16[2,256,1024]{2,1,0:T(8,128)(2,1)S(1)}, bf16[2,256,1024]{2,1,0:T(8,128)(2,1)S(1)}, bf16[2,256,1024...) custom-call(s32[6]{0:T(128)S(1)} %convert_reduce_fusion.1.meta, ...), custom_call_target="tpu_custom_call" | custom-call | flops 9663676416 | bytes 29360128 | tf_op jit(solution)/shard_map/attention/pallas_call | solution.py:187
  257.4 13.4 %collective-permute-start.17 = (bf16[2,256,1024]{2,1,0:T(8,128)(2,1)}, bf16[2,256,1024]{2,1,0:T(8,128)(2,1)}, u32[]{:S(2)}, u32[]{:S(2)}) collective-permute-start(bf16[2,256,1024]{2,1,0:T(8,128)(2,1)} %get-tuple-element.91), channel_id=1, source_target_pairs={{0,4},{1,5},{2,6},{3,7},{4,0},{5,1},{6,2},{7,3},{8,12},{9,13},{10,... | collective-permute-start | bytes 3145736 | tf_op jit(solution)/shard_map/ppermute | solution.py:261
  271.7 4.6 collective-permute-start.18
  276.3 12.2 %collective-permute-done.18.refs_2_ = bf16[2,128,1024]{2,1,0:T(8,128)(2,1)S(1)} collective-permute-done((bf16[2,128,1024]{2,1,0:T(8,128)(2,1)S(1)}, bf16[2,128,1024]{2,1,0:T(8,128)(2,1)S(1)}, u32[]{:S(2)}, u32[]{:S(2)}) %collective-permute-start.18) | collective-permute-done | bytes 524320 | tf_op jit(solution)/shard_map/ppermute | solution.py:261
  289.4 4.4 collective-permute-done.17
  299.9 2.1 collective-permute-start.22
  302.0 42.4 %collective-permute-done.22.refs_3_ = bf16[2,128,1024]{2,1,0:T(8,128)(2,1)S(1)} collective-permute-done((bf16[2,128,1024]{2,1,0:T(8,128)(2,1)S(1)}, bf16[2,128,1024]{2,1,0:T(8,128)(2,1)S(1)}, u32[]{:S(2)}, u32[]{:S(2)}) %collective-permute-start.22) | collective-permute-done | bytes 524320 | tf_op jit(solution)/shard_map/ppermute | solution.py:261
  345.3 2.4 add_convert_fusion.5
  355.6 42.6 %all_to_all.10 = bf16[16,8,1024]{2,1,0:T(8,128)(2,1)S(1)} all-to-all(bf16[16,8,1024]{2,1,0:T(8,128)(2,1)S(1)} %copy.24), channel_id=1, replica_groups=mesh['y'=4,'z_lo'=4,'x'=4,'z_hi'=2,'core'=2] {'z_lo','x'}, dimensions={0} | all-to-all | bytes 524288 | tf_op jit(solution)/shard_map/all_to_all | solution.py:363
  398.2 2.4 add_convert_fusion.3
  405.3 3.6 collective-permute-start.31
  408.9 2.2 collective-permute-start.30
  411.1 15.5 %collective-permute-done.27 = bf16[2,256,1024]{2,1,0:T(8,128)(2,1)S(1)} collective-permute-done((bf16[2,256,1024]{2,1,0:T(8,128)(2,1)S(1)}, bf16[2,256,1024]{2,1,0:T(8,128)(2,1)S(1)}, u32[]{:S(2)}, u32[]{:S(2)}) %collective-permute-start.27) | collective-permute-done | bytes 1048608 | tf_op jit(solution)/shard_map/ppermute | solution.py:261
  432.0 9.6 %collective-permute-done.31.refs_3_ = bf16[2,128,1024]{2,1,0:T(8,128)(2,1)S(1)} collective-permute-done((bf16[2,128,1024]{2,1,0:T(8,128)(2,1)S(1)}, bf16[2,128,1024]{2,1,0:T(8,128)(2,1)S(1)}, u32[]{:S(2)}, u32[]{:S(2)}) %collective-permute-start.31) | collective-permute-done | bytes 524320 | tf_op jit(solution)/shard_map/ppermute | solution.py:261
  441.6 11.3 %collective-permute-done.30.refs_2_ = bf16[2,128,1024]{2,1,0:T(8,128)(2,1)S(1)} collective-permute-done((bf16[2,128,1024]{2,1,0:T(8,128)(2,1)S(1)}, bf16[2,128,1024]{2,1,0:T(8,128)(2,1)S(1)}, u32[]{:S(2)}, u32[]{:S(2)}) %collective-permute-start.30) | collective-permute-done | bytes 524320 | tf_op jit(solution)/shard_map/ppermute | solution.py:261
  452.8 2.2 place.3
  (148 shorter events, 54.6 us)
Async XLA Ops:
  12.0 27.7 %collective-permute-start.3 = (bf16[2,256,1024]{2,1,0:T(8,128)(2,1)S(1)}, bf16[2,256,1024]{2,1,0:T(8,128)(2,1)S(1)}, u32[]{:S(2)}, u32[]{:S(2)}) collective-permute-start(bf16[2,256,1024]{2,1,0:T(8,128)(2,1)S(1)} %pad_maximum_fusion.refs_2_), channel_id=1, source_target_pairs={{0,4},{1,5},{2,6},{3,7},{4,8},{5,9},{6,10},{7,11},{8,12},{9,13},{1... | collective-permute-start | bytes 3145736 | tf_op jit(solution)/shard_map/ppermute | solution.py:261
  13.6 43.2 %collective-permute-start.4 = (bf16[2,256,1024]{2,1,0:T(8,128)(2,1)S(1)}, bf16[2,256,1024]{2,1,0:T(8,128)(2,1)}, u32[]{:S(2)}, u32[]{:S(2)}) collective-permute-start(bf16[2,256,1024]{2,1,0:T(8,128)(2,1)S(1)} %pad_maximum_fusion.refs_2_), channel_id=1, source_target_pairs={{0,12},{1,13},{2,14},{3,15},{4,0},{5,1},{6,2},{7,3},{8,4},{9,5},{1... | collective-permute-start | bytes 3145736 | tf_op jit(solution)/shard_map/ppermute | solution.py:261
  14.8 41.5 %all-to-all-start = ((bf16[16,8,1024]{2,1,0:T(8,128)(2,1)}), bf16[16,8,1024]{2,1,0:T(8,128)(2,1)S(1)}, u32[]{:S(2)}, u32[]{:S(2)}) async-start(bf16[16,8,1024]{2,1,0:T(8,128)(2,1)} %broadcast_in_dim.5), calls=%async_computation | async-start | bytes 524288 | tf_op jit(solution)/shard_map/all_to_all | solution.py:283
  23.3 127.6 %all-gather.3.cloned.1.call-start = ((), (), s32[]{:S(2)}) async-start(), calls=%async_computation.4 | async-start | bytes 1310720 | tf_op jit(solution)/shard_map/all_gather | solution.py:302
  23.3 39.9 %collective-permute-start.1 = (bf16[2,128,1024]{2,1,0:T(8,128)(2,1)}, bf16[2,128,1024]{2,1,0:T(8,128)(2,1)}, u32[]{:S(2)}, u32[]{:S(2)}) collective-permute-start(bf16[2,128,1024]{2,1,0:T(8,128)(2,1)} %get-tuple-element.127), channel_id=1, source_target_pairs={{0,3},{1,2},{2,1},{3,0},{4,7},{5,6},{6,5},{7,4},{8,11},{9,10},{10,... | collective-permute-start | bytes 1572872 | tf_op jit(solution)/shard_map/ppermute | solution.py:261
  26.5 48.4 %collective-permute-start = (bf16[2,128,1024]{2,1,0:T(8,128)(2,1)}, bf16[2,128,1024]{2,1,0:T(8,128)(2,1)}, u32[]{:S(2)}, u32[]{:S(2)}) collective-permute-start(bf16[2,128,1024]{2,1,0:T(8,128)(2,1)} %get-tuple-element.128), channel_id=1, source_target_pairs={{0,2},{1,3},{2,0},{3,1},{4,6},{5,7},{6,4},{7,5},{8,10},{9,11},{10,... | collective-permute-start | bytes 1572872 | tf_op jit(solution)/shard_map/ppermute | solution.py:261
  39.7 35.2 %collective-permute-start.5 = (bf16[2,256,1024]{2,1,0:T(8,128)(2,1)S(1)}, bf16[2,256,1024]{2,1,0:T(8,128)(2,1)}, u32[]{:S(2)}, u32[]{:S(2)}) collective-permute-start(bf16[2,256,1024]{2,1,0:T(8,128)(2,1)S(1)} %collective-permute-done.3.refs_4_), channel_id=1, source_target_pairs={{0,4},{1,5},{2,6},{3,7},{4,8},{5,9},{6,10},{7,11},{8,12},{9,13},{1... | collective-permute-start | bytes 3145736 | tf_op jit(solution)/shard_map/ppermute | solution.py:261
  59.1 57.8 %collective-permute-start.8 = (bf16[2,256,1024]{2,1,0:T(8,128)(2,1)}, bf16[2,256,1024]{2,1,0:T(8,128)(2,1)}, u32[]{:S(2)}, u32[]{:S(2)}) collective-permute-start(bf16[2,256,1024]{2,1,0:T(8,128)(2,1)} %broadcast_select_fusion.1), channel_id=1, source_target_pairs={{0,16},{1,17},{2,18},{3,19},{4,20},{5,21},{6,22},{7,23},{16,32},{1... | collective-permute-start | bytes 3145736 | tf_op jit(solution)/shard_map/ppermute | solution.py:261
  78.7 60.3 %collective-permute-start.7 = (bf16[2,256,1024]{2,1,0:T(8,128)(2,1)}, bf16[2,256,1024]{2,1,0:T(8,128)(2,1)S(1)}, u32[]{:S(2)}, u32[]{:S(2)}) collective-permute-start(bf16[2,256,1024]{2,1,0:T(8,128)(2,1)} %constant_dynamic-update-slice_fusion.refs_3_), channel_id=1, source_target_pairs={{0,12},{1,13},{2,14},{3,15},{4,0},{5,1},{6,2},{7,3},{8,4},{9,5},{1... | collective-permute-start | bytes 3145736 | tf_op jit(solution)/shard_map/ppermute | solution.py:261
  114.4 24.6 %collective-permute-start.6 = (bf16[2,256,1024]{2,1,0:T(8,128)(2,1)}, bf16[2,256,1024]{2,1,0:T(8,128)(2,1)S(1)}, u32[]{:S(2)}, u32[]{:S(2)}) collective-permute-start(bf16[2,256,1024]{2,1,0:T(8,128)(2,1)} %constant_dynamic-update-slice_fusion.refs_3_), channel_id=1, source_target_pairs={{0,4},{1,5},{2,6},{3,7},{4,8},{5,9},{6,10},{7,11},{8,12},{9,13},{1... | collective-permute-start | bytes 3145736 | tf_op jit(solution)/shard_map/ppermute | solution.py:261
  116.8 177.0 %reduce-scatter.2.cloned.1.call-start = ((), (), s32[]{:S(2)}) async-start(), calls=%async_computation.3 | async-start | bytes 1310720 | tf_op jit(solution)/shard_map/reduce_scatter | solution.py:321
  140.2 54.5 %collective-permute-start.11 = (bf16[2,256,1024]{2,1,0:T(8,128)(2,1)}, bf16[2,256,1024]{2,1,0:T(8,128)(2,1)}, u32[]{:S(2)}, u32[]{:S(2)}) collective-permute-start(bf16[2,256,1024]{2,1,0:T(8,128)(2,1)} %broadcast_select_fusion), channel_id=1, source_target_pairs={{0,16},{1,17},{2,18},{3,19},{4,20},{5,21},{6,22},{7,23},{16,32},{1... | collective-permute-start | bytes 3145736 | tf_op jit(solution)/shard_map/ppermute | solution.py:261
  142.9 51.8 %collective-permute-start.14 = (bf16[2,256,1024]{2,1,0:T(8,128)(2,1)}, bf16[2,256,1024]{2,1,0:T(8,128)(2,1)}, u32[]{:S(2)}, u32[]{:S(2)}) collective-permute-start(bf16[2,256,1024]{2,1,0:T(8,128)(2,1)} %collective-permute-done.8.refs_12_), channel_id=1, source_target_pairs={{0,4},{1,5},{2,6},{3,7},{4,0},{5,1},{6,2},{7,3},{8,12},{9,13},{10,... | collective-permute-start | bytes 3145736 | tf_op jit(solution)/shard_map/ppermute | solution.py:261
  145.9 48.8 %collective-permute-start.13 = (bf16[2,256,1024]{2,1,0:T(8,128)(2,1)S(1)}, bf16[2,256,1024]{2,1,0:T(8,128)(2,1)}, u32[]{:S(2)}, u32[]{:S(2)}) collective-permute-start(bf16[2,256,1024]{2,1,0:T(8,128)(2,1)S(1)} %collective-permute-done.7.refs_7_), channel_id=1, source_target_pairs={{0,12},{1,13},{2,14},{3,15},{4,0},{5,1},{6,2},{7,3},{8,4},{9,5},{1... | collective-permute-start | bytes 3145736 | tf_op jit(solution)/shard_map/ppermute | solution.py:261
  147.0 47.7 %collective-permute-start.12 = (bf16[2,128,1024]{2,1,0:T(8,128)(2,1)S(1)}, bf16[2,128,1024]{2,1,0:T(8,128)(2,1)S(1)}, u32[]{:S(2)}, u32[]{:S(2)}) collective-permute-start(bf16[2,128,1024]{2,1,0:T(8,128)(2,1)S(1)} %pad_maximum_fusion.4), channel_id=1, source_target_pairs={{0,2},{1,3},{2,0},{3,1},{4,6},{5,7},{6,4},{7,5},{8,10},{9,11},{10,... | collective-permute-start | bytes 1572872 | tf_op jit(solution)/shard_map/ppermute | solution.py:261
  150.8 49.9 %collective-permute-start.10 = (bf16[2,128,1024]{2,1,0:T(8,128)(2,1)S(1)}, bf16[2,128,1024]{2,1,0:T(8,128)(2,1)}, u32[]{:S(2)}, u32[]{:S(2)}) collective-permute-start(bf16[2,128,1024]{2,1,0:T(8,128)(2,1)S(1)} %pad_maximum_fusion.3), channel_id=1, source_target_pairs={{0,1},{1,0},{2,3},{3,2},{4,5},{5,4},{6,7},{7,6},{8,9},{9,8},{10,11... | collective-permute-start | bytes 1572872 | tf_op jit(solution)/shard_map/ppermute | solution.py:261
  194.7 28.4 %collective-permute-start.15 = (bf16[2,256,1024]{2,1,0:T(8,128)(2,1)}, bf16[2,256,1024]{2,1,0:T(8,128)(2,1)S(1)}, u32[]{:S(2)}, u32[]{:S(2)}) collective-permute-start(bf16[2,256,1024]{2,1,0:T(8,128)(2,1)} %collective-permute-done.11.refs_13_), channel_id=1, source_target_pairs={{0,4},{1,5},{2,6},{3,7},{4,0},{5,1},{6,2},{7,3},{8,12},{9,13},{10,... | collective-permute-start | bytes 3145736 | tf_op jit(solution)/shard_map/ppermute | solution.py:261
  257.4 36.3 %collective-permute-start.17 = (bf16[2,256,1024]{2,1,0:T(8,128)(2,1)}, bf16[2,256,1024]{2,1,0:T(8,128)(2,1)}, u32[]{:S(2)}, u32[]{:S(2)}) collective-permute-start(bf16[2,256,1024]{2,1,0:T(8,128)(2,1)} %get-tuple-element.91), channel_id=1, source_target_pairs={{0,4},{1,5},{2,6},{3,7},{4,0},{5,1},{6,2},{7,3},{8,12},{9,13},{10,... | collective-permute-start | bytes 3145736 | tf_op jit(solution)/shard_map/ppermute | solution.py:261
  295.9 49.4 %collective-permute-start.19 = (bf16[2,256,1024]{2,1,0:T(8,128)(2,1)S(1)}, bf16[2,256,1024]{2,1,0:T(8,128)(2,1)S(1)}, u32[]{:S(2)}, u32[]{:S(2)}) collective-permute-start(bf16[2,256,1024]{2,1,0:T(8,128)(2,1)S(1)} %add_convert_fusion.7), channel_id=1, source_target_pairs={{8,24},{9,25},{10,26},{11,27},{12,28},{13,29},{14,30},{15,31},{16,... | collective-permute-start | bytes 3145736 | tf_op jit(solution)/shard_map/ppermute | solution.py:261
  297.8 47.5 %collective-permute-start.20 = (bf16[2,256,1024]{2,1,0:T(8,128)(2,1)}, bf16[2,256,1024]{2,1,0:T(8,128)(2,1)S(1)}, u32[]{:S(2)}, u32[]{:S(2)}) collective-permute-start(bf16[2,256,1024]{2,1,0:T(8,128)(2,1)} %get-tuple-element.99), channel_id=1, source_target_pairs={{0,4},{1,5},{2,6},{3,7},{4,8},{5,9},{6,10},{7,11},{8,12},{9,13},{1... | collective-permute-start | bytes 3145736 | tf_op jit(solution)/shard_map/ppermute | solution.py:261
  297.9 47.4 %collective-permute-start.21 = (bf16[2,256,1024]{2,1,0:T(8,128)(2,1)}, bf16[2,256,1024]{2,1,0:T(8,128)(2,1)S(1)}, u32[]{:S(2)}, u32[]{:S(2)}) collective-permute-start(bf16[2,256,1024]{2,1,0:T(8,128)(2,1)} %get-tuple-element.100), channel_id=1, source_target_pairs={{0,4},{1,5},{2,6},{3,7},{4,0},{5,1},{6,2},{7,3},{8,12},{9,13},{10,... | collective-permute-start | bytes 3145736 | tf_op jit(solution)/shard_map/ppermute | solution.py:261
  299.9 44.5 %collective-permute-start.22 = (bf16[2,128,1024]{2,1,0:T(8,128)(2,1)S(1)}, bf16[2,128,1024]{2,1,0:T(8,128)(2,1)S(1)}, u32[]{:S(2)}, u32[]{:S(2)}) collective-permute-start(bf16[2,128,1024]{2,1,0:T(8,128)(2,1)S(1)} %copy-done.26), channel_id=1, source_target_pairs={{0,3},{1,2},{2,1},{3,0},{4,7},{5,6},{6,5},{7,4},{8,11},{9,10},{10,... | collective-permute-start | bytes 1572872 | tf_op jit(solution)/shard_map/ppermute | solution.py:261
  347.7 50.5 %collective-permute-start.24 = (bf16[2,256,1024]{2,1,0:T(8,128)(2,1)}, bf16[2,256,1024]{2,1,0:T(8,128)(2,1)}, u32[]{:S(2)}, u32[]{:S(2)}) collective-permute-start(bf16[2,256,1024]{2,1,0:T(8,128)(2,1)} %get-tuple-element.135), channel_id=1, source_target_pairs={{0,12},{1,13},{2,14},{3,15},{4,0},{5,1},{6,2},{7,3},{8,4},{9,5},{1... | collective-permute-start | bytes 3145736 | tf_op jit(solution)/shard_map/ppermute | solution.py:261
  348.9 49.3 %collective-permute-start.23 = (bf16[2,256,1024]{2,1,0:T(8,128)(2,1)}, bf16[2,256,1024]{2,1,0:T(8,128)(2,1)}, u32[]{:S(2)}, u32[]{:S(2)}) collective-permute-start(bf16[2,256,1024]{2,1,0:T(8,128)(2,1)} %get-tuple-element.136), channel_id=1, source_target_pairs={{0,4},{1,5},{2,6},{3,7},{4,8},{5,9},{6,10},{7,11},{8,12},{9,13},{1... | collective-permute-start | bytes 3145736 | tf_op jit(solution)/shard_map/ppermute | solution.py:261
  351.1 47.1 %collective-permute-start.25 = (bf16[2,256,1024]{2,1,0:T(8,128)(2,1)}, bf16[2,256,1024]{2,1,0:T(8,128)(2,1)}, u32[]{:S(2)}, u32[]{:S(2)}) collective-permute-start(bf16[2,256,1024]{2,1,0:T(8,128)(2,1)} %add_convert_fusion.4), channel_id=1, source_target_pairs={{8,24},{9,25},{10,26},{11,27},{12,28},{13,29},{14,30},{15,31},{16,... | collective-permute-start | bytes 3145736 | tf_op jit(solution)/shard_map/ppermute | solution.py:261
  353.0 45.2 %collective-permute-start.26 = (bf16[2,256,1024]{2,1,0:T(8,128)(2,1)}, bf16[2,256,1024]{2,1,0:T(8,128)(2,1)}, u32[]{:S(2)}, u32[]{:S(2)}) collective-permute-start(bf16[2,256,1024]{2,1,0:T(8,128)(2,1)} %get-tuple-element.114), channel_id=1, source_target_pairs={{0,12},{1,13},{2,14},{3,15},{4,0},{5,1},{6,2},{7,3},{8,4},{9,5},{1... | collective-permute-start | bytes 3145736 | tf_op jit(solution)/shard_map/ppermute | solution.py:261
  400.6 26.0 %collective-permute-start.27 = (bf16[2,256,1024]{2,1,0:T(8,128)(2,1)S(1)}, bf16[2,256,1024]{2,1,0:T(8,128)(2,1)S(1)}, u32[]{:S(2)}, u32[]{:S(2)}) collective-permute-start(bf16[2,256,1024]{2,1,0:T(8,128)(2,1)S(1)} %get-tuple-element.133), channel_id=1, source_target_pairs={{0,4},{1,5},{2,6},{3,7},{4,8},{5,9},{6,10},{7,11},{8,12},{9,13},{1... | collective-permute-start | bytes 3145736 | tf_op jit(solution)/shard_map/ppermute | solution.py:261
  400.7 26.7 %collective-permute-start.28 = (bf16[2,256,1024]{2,1,0:T(8,128)(2,1)S(1)}, bf16[2,256,1024]{2,1,0:T(8,128)(2,1)S(1)}, u32[]{:S(2)}, u32[]{:S(2)}) collective-permute-start(bf16[2,256,1024]{2,1,0:T(8,128)(2,1)S(1)} %get-tuple-element.134), channel_id=1, source_target_pairs={{0,12},{1,13},{2,14},{3,15},{4,0},{5,1},{6,2},{7,3},{8,4},{9,5},{1... | collective-permute-start | bytes 3145736 | tf_op jit(solution)/shard_map/ppermute | solution.py:261
  402.8 26.5 %collective-permute-start.16 = (bf16[2,128,1024]{2,1,0:T(8,128)(2,1)S(1)}, bf16[2,128,1024]{2,1,0:T(8,128)(2,1)S(1)}, u32[]{:S(2)}, u32[]{:S(2)}) collective-permute-start(bf16[2,128,1024]{2,1,0:T(8,128)(2,1)S(1)} %get-tuple-element.139), channel_id=1, source_target_pairs={{0,1},{1,0},{2,3},{3,2},{4,5},{5,4},{6,7},{7,6},{8,9},{9,8},{10,11... | collective-permute-start | bytes 1572872 | tf_op jit(solution)/shard_map/ppermute | solution.py:261
  405.3 36.2 %collective-permute-start.31 = (bf16[2,128,1024]{2,1,0:T(8,128)(2,1)S(1)}, bf16[2,128,1024]{2,1,0:T(8,128)(2,1)S(1)}, u32[]{:S(2)}, u32[]{:S(2)}) collective-permute-start(bf16[2,128,1024]{2,1,0:T(8,128)(2,1)S(1)} %get-tuple-element.129), channel_id=1, source_target_pairs={{0,3},{1,2},{2,1},{3,0},{4,7},{5,6},{6,5},{7,4},{8,11},{9,10},{10,... | collective-permute-start | bytes 1572872 | tf_op jit(solution)/shard_map/ppermute | solution.py:261
  408.9 43.9 %collective-permute-start.30 = (bf16[2,128,1024]{2,1,0:T(8,128)(2,1)S(1)}, bf16[2,128,1024]{2,1,0:T(8,128)(2,1)S(1)}, u32[]{:S(2)}, u32[]{:S(2)}) collective-permute-start(bf16[2,128,1024]{2,1,0:T(8,128)(2,1)S(1)} %get-tuple-element.130), channel_id=1, source_target_pairs={{0,2},{1,3},{2,0},{3,1},{4,6},{5,7},{6,4},{7,5},{8,10},{9,11},{10,... | collective-permute-start | bytes 1572872 | tf_op jit(solution)/shard_map/ppermute | solution.py:261
  429.0 23.9 %collective-permute-start.29 = (bf16[2,128,1024]{2,1,0:T(8,128)(2,1)}, bf16[2,128,1024]{2,1,0:T(8,128)(2,1)S(1)}, u32[]{:S(2)}, u32[]{:S(2)}) collective-permute-start(bf16[2,128,1024]{2,1,0:T(8,128)(2,1)} %get-tuple-element.131), channel_id=1, source_target_pairs={{0,1},{1,0},{2,3},{3,2},{4,5},{5,4},{6,7},{7,6},{8,9},{9,8},{10,11... | collective-permute-start | bytes 1572872 | tf_op jit(solution)/shard_map/ppermute | solution.py:261
  (34 other events, 838.4 us)
Sparse Core Ops, SparseCore 0:
  116.9 32.4 all-gather.2
  223.3 26.0 reduce-scatter.1
